TPU v7x, 256 devices: a whole 4x4x8 slice. The times are simulated.
256 devices in a mesh: rep: 16 (over z_hi, y), zero: 16 (over z_lo, x, core).
Axes of the slice: x: 4, y: 4, z: 8 (z_hi: 4, z_lo: 2; z = z_hi * 2 + z_lo), core: 2. Of those that a mesh axis runs over, the one named last changes fastest.
Arguments:
- tokens: bfloat16 [256, 6144], P(None, 'zero'), may hold values from -6 to 6
- gate_weight: bfloat16 [6144, 14336], P('zero', 'rep'), may hold values from -0.078125 to 0.078125
- up_weight: bfloat16 [6144, 14336], P('zero', 'rep'), may hold values from -0.078125 to 0.078125
- down_weight: bfloat16 [14336, 6144], P('rep', 'zero'), may hold values from -0.046875 to 0.046875
- gate_scale: float32 [6144], P('zero'), may hold values from 0.5 to 2
- up_scale: float32 [6144], P('zero'), may hold values from 0.5 to 2
- down_scale: float32 [14336], P('rep'), may hold values from 0.5 to 2
- gate_probe: bfloat16 [6144, 14336], P('zero', 'rep'), may hold values from -1 to 1, as said below
- up_probe: bfloat16 [6144, 14336], P('zero', 'rep'), may hold values from -1 to 1, as said below
- down_probe: bfloat16 [14336, 6144], P('rep', 'zero'), may hold values from -1 to 1, as said below
Outputs:
- gate_gradient: float32 [6144, 14336], P('zero', 'rep')
- up_gradient: float32 [6144, 14336], P('zero', 'rep')
- down_gradient: float32 [14336, 6144], P('rep', 'zero')
- gate_hessian: float32 [6144, 14336], P('zero', 'rep')
- up_hessian: float32 [6144, 14336], P('zero', 'rep')
- down_hessian: float32 [14336, 6144], P('rep', 'zero')
Inputs may be any that keep to these rules, and one draw needn't show every extreme that they name: `gate_probe`: every entry is +1 or -1. `up_probe`: every entry is +1 or -1. `down_probe`: every entry is +1 or -1.
All inputs are finite; a program needn't handle non-finite values.
Results may differ from a plain program's by a relative error of at most 0.0075.
Values may be sent and summed in bfloat16 or wider, within the bound.
A program may use at most 64 MiB of HBM per device.

v0:
```python
import jax
import jax.numpy as jnp
from jax import lax
from jax.sharding import PartitionSpec as P

D = 6144
H = 14336


def matmul(left, right):
    return jnp.dot(left, right, preferred_element_type=jnp.float32)


def matmul_last(left, right):
    return lax.dot_general(
        left, right, (((1,), (1,)), ((), ())), preferred_element_type=jnp.float32
    )


def contract_rows(left, right):
    return lax.dot_general(
        left, right, (((0,), (0,)), ((), ())), preferred_element_type=jnp.float32
    )


def dequantize(codes, scales):
    return (codes.astype(jnp.float32) * scales[:, None]).astype(jnp.bfloat16)


def silu_parts(gate_pre):
    logistic = jax.nn.sigmoid(gate_pre)
    activated = gate_pre * logistic
    slope = logistic * (1.0 + gate_pre * (1.0 - logistic))
    bend = logistic * (1.0 - logistic) * (2.0 + gate_pre * (1.0 - 2.0 * logistic))
    return (activated, slope, bend)


def local(
    tokens,
    gate_weight,
    up_weight,
    down_weight,
    gate_scale,
    up_scale,
    down_scale,
    gate_probe,
    up_probe,
    down_probe,
):
    row_count = tokens.shape[0]
    hidden = gate_weight.shape[1]
    factor = float(row_count) ** (-0.5)
    feature_factor = float(D) ** (-0.5)
    hidden_factor = float(H) ** (-0.5)
    gate_matrix = dequantize(gate_weight, gate_scale)
    up_matrix = dequantize(up_weight, up_scale)
    down_matrix = dequantize(down_weight, down_scale)
    gate_pre, up_pre, gate_tan, up_tan = lax.psum(
        (
            matmul(tokens, gate_matrix),
            matmul(tokens, up_matrix),
            feature_factor * matmul(tokens, gate_probe),
            feature_factor * matmul(tokens, up_probe),
        ),
        "zero",
    )
    activated, slope, bend = silu_parts(gate_pre)
    hidden_act = (activated * up_pre).astype(jnp.bfloat16)
    tangent_act = (slope * gate_tan * up_pre + activated * up_tan).astype(jnp.bfloat16)
    output_part = matmul(hidden_act, down_matrix)
    output_tan_part = hidden_factor * matmul(hidden_act, down_probe) + matmul(
        tangent_act, down_matrix
    )
    output, output_tan = lax.psum((output_part, output_tan_part), "rep")
    back = (factor * (tokens.astype(jnp.float32) + output)).astype(jnp.bfloat16)
    back_tan = (factor * output_tan).astype(jnp.bfloat16)
    hid_back, hid_back_tan = lax.psum(
        (
            matmul_last(back, down_matrix),
            matmul_last(back_tan, down_matrix) + hidden_factor * matmul_last(back, down_probe),
        ),
        "zero",
    )
    gate_back = (hid_back * up_pre * slope).astype(jnp.bfloat16)
    up_back = (hid_back * activated).astype(jnp.bfloat16)
    gate_back_tan = (
        hid_back_tan * up_pre * slope + hid_back * (up_tan * slope + up_pre * bend * gate_tan)
    ).astype(jnp.bfloat16)
    up_back_tan = (hid_back_tan * activated + hid_back * slope * gate_tan).astype(jnp.bfloat16)
    left_side = jnp.concatenate([gate_back, up_back, gate_back_tan, up_back_tan], axis=1)
    square = contract_rows(tokens, left_side)
    down_gradient = contract_rows(hidden_act, back)
    down_hessian = contract_rows(tangent_act, back) + contract_rows(hidden_act, back_tan)
    gate_gradient = square[:, 0:hidden]
    up_gradient = square[:, hidden : 2 * hidden]
    gate_hessian = square[:, 2 * hidden : 3 * hidden]
    up_hessian = square[:, 3 * hidden : 4 * hidden]
    return (gate_gradient, up_gradient, down_gradient, gate_hessian, up_hessian, down_hessian)


def solution(mesh):
    in_specs = (
        P(None, "zero"),
        P("zero", "rep"),
        P("zero", "rep"),
        P("rep", "zero"),
        P("zero"),
        P("zero"),
        P("rep"),
        P("zero", "rep"),
        P("zero", "rep"),
        P("rep", "zero"),
    )
    out_specs = (
        P("zero", "rep"),
        P("zero", "rep"),
        P("rep", "zero"),
        P("zero", "rep"),
        P("zero", "rep"),
        P("rep", "zero"),
    )
    return jax.shard_map(local, mesh=mesh, in_specs=in_specs, out_specs=out_specs, check_vma=False)
```

profile of v0, /device:TPU:1, one launch (start us, length us, event | category | flops | bytes accessed | tf_op | source)
XLA Modules:
  0.0 477.0 jit_solution(8670467627339298993)
XLA Ops:
  7.2 0.0 all-reduce.9.cloned.1.call-start
  7.3 2.7 convolution_multiply_fusion.2
  10.0 1.4 convolution_multiply_fusion.1
  11.4 1.5 convolution_bitcast_fusion.1
  12.8 1.5 convolution_bitcast_fusion.2
  14.3 0.0 all-reduce.9.cloned.1.call-update
  14.3 0.0 all-reduce.11.cloned.1.call-start
  14.4 136.0 %all-reduce.9.cloned.1.call-done = (f32[256,896]{0,1:T(8,128)}, f32[256,896]{0,1:T(8,128)}, f32[256,896]{0,1:T(8,128)}, f32[256,896]{0,1:T(8,128)}) async-done(((f32[256,896]{0,1:T(8,128)}, f32[256,896]{0,1:T(8,128)}, f32[256,896]{0,1:T(8,128)}, f32[256,896]{0,1:T(8,128)}), (f32[256,896]{0,1:T(8,128)}, f32[256,896]{0,1:T(8,128)}, f32[256,896]{0,1:T(8,128)}, ...) | async-done | bytes 3670032 | tf_op jit(solution)/shard_map/psum | solution.py:58
  150.4 2.5 add_convert_fusion.1
  152.9 0.5 convolution_multiply_fusion.3
  153.4 0.6 copy-done.1
  154.0 1.3 fusion.25
  155.3 1.3 convolution_add_fusion.1
  156.6 0.0 all-reduce.11.cloned.1.call-update
  156.6 0.0 all-reduce.7.cloned.1.call-start
  156.6 158.9 %all-reduce.11.cloned.1.call-done = (f32[256,384]{1,0:T(8,128)}, f32[256,384]{1,0:T(8,128)}) async-done(((f32[256,384]{1,0:T(8,128)}, f32[256,384]{1,0:T(8,128)}), (f32[256,384]{1,0:T(8,128)}, f32[256,384]{1,0:T(8,128)})) %all-reduce.11.cloned.1.call-update) | async-done | bytes 786448 | tf_op jit(solution)/shard_map/psum | solution.py:74
  315.5 1.1 multiply_convert_fusion.9
  316.6 1.4 fusion.24
  318.0 0.4 fusion.20
  318.5 1.4 fusion.7
  319.8 0.0 all-reduce.7.cloned.1.call-update
  319.8 1.5 fusion.27
  321.3 0.4 fusion.28
  321.7 1.5 convolution_add_fusion
  323.2 132.3 %all-reduce.7.cloned.1.call-done = (f32[256,896]{0,1:T(8,128)}, f32[256,896]{0,1:T(8,128)}) async-done(((f32[256,896]{0,1:T(8,128)}, f32[256,896]{0,1:T(8,128)}), (f32[256,896]{0,1:T(8,128)}, f32[256,896]{0,1:T(8,128)})) %all-reduce.7.cloned.1.call-update) | async-done | bytes 1835024 | tf_op jit(solution)/shard_map/psum | solution.py:77
  455.5 3.3 fusion.16
  458.8 1.1 convolution_bitcast_fusion
  459.9 1.9 fusion.26
  461.8 2.9 copy.21
  464.6 2.9 copy.22
  467.5 1.5 copy.23
  469.0 1.5 copy.24
  (21 shorter events, 0.1 us)
Async XLA Ops:
  7.2 145.8 %copy-start = (bf16[896,384]{1,0:T(8,128)(2,1)S(1)}, bf16[896,384]{1,0:T(8,128)(2,1)}, u32[]{:S(2)}) copy-start(bf16[896,384]{1,0:T(8,128)(2,1)} %param.19) | copy-start | bytes 2064388
  7.2 2.8 copy-start.2
  7.2 2.8 copy-start.5
  7.2 4.2 copy-start.6
  7.2 4.2 copy-start.9
  7.2 143.2 %all-reduce.9.cloned.1.call-start = ((), (), s32[]{:S(2)}) async-start(), calls=%async_computation.1 | async-start | bytes 7340032 | tf_op jit(solution)/shard_map/psum | solution.py:58
  10.0 2.9 copy-start.7
  10.0 2.9 copy-start.10
  14.3 301.2 %all-reduce.11.cloned.1.call-start = ((), (), s32[]{:S(2)}) async-start(), calls=%async_computation.2 | async-start | bytes 1572864 | tf_op jit(solution)/shard_map/psum | solution.py:74
  152.9 1.1 copy-start.1
  152.9 1.1 copy-start.8
  156.6 298.9 %all-reduce.7.cloned.1.call-start = ((), (), s32[]{:S(2)}) async-start(), calls=%async_computation | async-start | bytes 3670016 | tf_op jit(solution)/shard_map/psum | solution.py:77
  315.5 2.5 copy-start.4
  321.7 133.8 %copy-start.3 = (f32[256,896]{0,1:T(8,128)S(1)}, f32[256,896]{0,1:T(8,128)}, u32[]{:S(2)}) copy-start(f32[256,896]{0,1:T(8,128)} %get-tuple-element.14) | copy-start | bytes 2752516
Sparse Core Ops, SparseCore 0:
  14.4 135.9 all-reduce.8
  156.7 158.7 all-reduce.10
  320.0 135.4 all-reduce.6
where the time goes:
time: 477 us
  waiting for transfers between devices  427 us (90%)
  matrix products  17.7 us (4%)
  between operations  13.9 us (3%)
  local copies, waits for them, and re-layouts  11.3 us (2%)
  other arithmetic  6.83 us (1%)
    psum x1, waiting for transfers between devices, local(): output, output_tan = lax.psum((output_part, output_tan_part), 'rep')  159 us
    psum x1, waiting for transfers between devices, local(): lax.psum((matmul(tokens, gate_matrix), matmul(tokens, up_matrix), feature...  136 us
    psum x1, waiting for transfers between devices, local(): lax.psum((matmul_last(back, down_matrix), matmul_last(back_tan, down_matr...  132 us
    dot_general x7, matrix products, matmul(): return jnp.dot(left, right, preferred_element_type=jnp.float32)  10 us
  transfers between devices with their start and end apart: 3, of which 3 were waited for; matrix products, arithmetic and copies ran while one was open for 1% of the time, Pallas kernels for 0%

commit v1 on v0

v1 whole, which is shorter than its diff:
```python
import functools

import jax
import jax.numpy as jnp
from jax import lax
from jax.experimental import pallas as pl
from jax.experimental.pallas import tpu as pltpu
from jax.sharding import PartitionSpec as P

D = 6144
H = 14336
TOKENS = 256

DL = 384
HL = 896
CHIPS = 8
REPS = 16
CHUNKS = 2
ROWS = 8

BF16 = jnp.bfloat16
F32 = jnp.float32
MESH = pl.DeviceIdType.MESH

ZERO_STEPS = tuple((dz, dx) for dz in range(2) for dx in range(4) if dz or dx)
REP_STEPS = tuple((dz, dy) for dz in range(4) for dy in range(4) if dz or dy)


def dot(left, right):
    return jnp.dot(left, right, preferred_element_type=F32)


def dot_last(left, right):
    return lax.dot_general(left, right, (((1,), (1,)), ((), ())), preferred_element_type=F32)


def dot_rows(left, right):
    return lax.dot_general(left, right, (((0,), (0,)), ((), ())), preferred_element_type=F32)


def pair(first, second):
    width = first.shape[-1]
    return jnp.concatenate([first.reshape(-1, ROWS, width), second.reshape(-1, ROWS, width)], axis=1).astype(BF16)


def exchange_kernel(
    tok_hbm, gw_hbm, uw_hbm, dw_hbm, gp_hbm, up_hbm, dp_hbm, gs_ref, us_ref, ds_ref,
    g_ref, x_ref, y_ref,
    tok, tok_sib, tok_order, gw, uw, gp, up, dw, dm, dp,
    sib_out, sib_in, own, stage, landed, mult,
    outs, outs_in, back, hid, hid_own, hid_in,
    load_sem, pre_s, pre_r, sib_s, sib_r, rs_s, rs_r, ag_s, ag_r, xs_s, xs_r,
    rep_s, rep_r, repag_s, repag_r, ys_s, ys_r, rs2_s, rs2_r, ag4_s, ag4_r, fw_s, fw_r,
):
    rep = lax.axis_index("rep")
    zero = lax.axis_index("zero")
    core = zero % 2
    chip = zero // 2
    z_lo, x = chip // 4, chip % 4
    z_hi, y = rep // 4, rep % 4
    sibling = (rep, chip * 2 + (1 - core))
    chips = [((z_lo + dz) % 2) * 4 + (x + dx) % 4 for dz, dx in ZERO_STEPS]
    chips_from = [((z_lo + dz) % 2) * 4 + (x + 4 - dx) % 4 for dz, dx in ZERO_STEPS]
    reps = [((z_hi + dz) % 4) * 4 + (y + dy) % 4 for dz, dy in REP_STEPS]

    def remote(src, dst, send, recv, device):
        return pltpu.make_async_remote_copy(
            src_ref=src, dst_ref=dst, send_sem=send, recv_sem=recv, device_id=device, device_id_type=MESH
        )

    barrier = pltpu.get_barrier_semaphore()
    pl.semaphore_signal(barrier, inc=1, device_id=sibling, device_id_type=MESH)
    for other in chips:
        pl.semaphore_signal(barrier, inc=1, device_id=(rep, other * 2 + core), device_id_type=MESH)
    for other in reps:
        pl.semaphore_signal(barrier, inc=1, device_id=(other, zero), device_id_type=MESH)

    loads = [
        pltpu.make_async_copy(src, dst, load_sem.at[n])
        for n, (src, dst) in enumerate(
            ((tok_hbm, tok), (gp_hbm, gp), (up_hbm, up), (gw_hbm, gw), (uw_hbm, uw), (dw_hbm, dw), (dp_hbm, dp.at[0]))
        )
    ]
    for copy in loads:
        copy.start()

    loads[0].wait()
    tok_order[0:128, :] = tok[pl.ds(pl.multiple_of((1 - core) * 128, 128), 128), :]
    tok_order[128:256, :] = tok[pl.ds(pl.multiple_of(core * 128, 128), 128), :]
    tokens = tok_order[...]

    def scaled(ref, scale_ref, out_ref, index=None):
        rows, width = ref.shape
        column = jnp.broadcast_to(scale_ref[...], (128, rows)).T
        for n in range(width // 128):
            block = (ref[:, n * 128 : (n + 1) * 128].astype(F32) * column).astype(BF16)
            if index is None:
                out_ref[:, n * 128 : (n + 1) * 128] = block
            else:
                out_ref[index, :, n * 128 : (n + 1) * 128] = block

    sib_copies = {}

    def pre(p, first, second):
        a = dot(tokens, first)
        b = dot(tokens, second)
        own[2 * p] = a[128:256]
        own[2 * p + 1] = b[128:256]
        both = pair(a[0:128], b[0:128])
        for q in range(CHUNKS):
            sib_out[q, p] = both[q * CHIPS : (q + 1) * CHIPS]
        for q in range(CHUNKS):
            copy = remote(sib_out.at[q, p], sib_in.at[q, p], sib_s.at[q, p], sib_r.at[q, p], sibling)
            sib_copies[q, p] = copy

    loads[1].wait()
    loads[2].wait()
    pre(0, gp[...], up[...])
    pl.semaphore_wait(barrier, 1 + len(chips) + len(reps))
    for q in range(CHUNKS):
        sib_copies[q, 0].start()
    loads[3].wait()
    scaled(gw, gs_ref, gw)
    loads[4].wait()
    scaled(uw, us_ref, uw)
    pre(1, gw[...], uw[...])
    for q in range(CHUNKS):
        sib_copies[q, 1].start()

    rs_copies = {}
    for q in range(CHUNKS):
        for p in range(2):
            sib_copies[q, p].wait_recv()
            a = own[2 * p, q * 64 : (q + 1) * 64].reshape(CHIPS, ROWS, HL)
            b = own[2 * p + 1, q * 64 : (q + 1) * 64].reshape(CHIPS, ROWS, HL)
            both = jnp.concatenate([a, b], axis=1) + sib_in[q, p].astype(F32)
            stage[q, :, p * 16 : (p + 1) * 16, :] = both.astype(BF16)
        for k, other in enumerate(chips):
            copy = remote(stage.at[q, other], landed.at[q, k], rs_s.at[q, k], rs_r.at[q, k], (rep, other * 2 + core))
            copy.start()
            rs_copies[q, k] = copy

    pre_copies = [
        remote(tok.at[pl.ds(pl.multiple_of((1 - core) * 128, 128), 128)], tok_sib, pre_s.at[0], pre_r.at[0], sibling)
    ]
    pre_copies[0].start()
    loads[5].wait()
    scaled(dw, ds_ref, dm, 0)
    loads[6].wait()
    pre_copies.append(remote(dm.at[0], dm.at[1], pre_s.at[1], pre_r.at[1], sibling))
    pre_copies.append(remote(dp.at[0], dp.at[1], pre_s.at[2], pre_r.at[2], sibling))
    pre_copies[1].start()
    pre_copies[2].start()

    feature_factor = float(D) ** -0.5
    hidden_factor = float(H) ** -0.5
    factor = float(TOKENS) ** -0.5

    ag_copies = {}
    for q in range(CHUNKS):
        row = pl.multiple_of(q * 64 + chip * ROWS, ROWS)
        total = [own[n, pl.ds(row, ROWS), :] for n in range(4)]
        for p in range(2):
            part = sib_in[q, p, chip].astype(F32)
            total[2 * p] += part[0:8]
            total[2 * p + 1] += part[8:16]
        for k in range(len(chips)):
            rs_copies[q, k].wait_recv()
            for p in range(2):
                part = landed[q, k, p * 16 : (p + 1) * 16, :].astype(F32)
                total[2 * p] += part[0:8]
                total[2 * p + 1] += part[8:16]
        gate_tan, up_tan, gate_pre, up_pre = total
        gate_tan = feature_factor * gate_tan
        up_tan = feature_factor * up_tan
        logistic = jax.nn.sigmoid(gate_pre)
        act = gate_pre * logistic
        slope = logistic * (1.0 + gate_pre * (1.0 - logistic))
        bend = logistic * (1.0 - logistic) * (2.0 + gate_pre * (1.0 - 2.0 * logistic))
        lean = slope * gate_tan
        x_ref[core, q, chip] = jnp.concatenate([act * up_pre, lean * up_pre + act * up_tan], axis=0).astype(BF16)
        for k, other in enumerate(chips):
            copy = remote(
                x_ref.at[core, q, chip], x_ref.at[core, q, chip], ag_s.at[q, k], ag_r.at[q, k], (rep, other * 2 + core)
            )
            copy.start()
            ag_copies[q, k] = copy
        mult[q, 0] = up_pre * slope
        mult[q, 1] = act
        mult[q, 2] = up_tan * slope + up_pre * bend * gate_tan
        mult[q, 3] = lean

    for copy in pre_copies:
        copy.wait_recv()
    xs_copies = []
    rep_copies = {}
    for q in range(CHUNKS):
        for k in range(len(chips)):
            ag_copies[q, k].wait_recv()
        copy = remote(x_ref.at[core, q], x_ref.at[core, q], xs_s.at[q], xs_r.at[q], sibling)
        copy.start()
        xs_copies.append(copy)
        hidden = x_ref[core, q].reshape(CHIPS * 16, HL)
        for f in range(2):
            straight = dot(hidden, dm[f]).reshape(CHIPS, 2, ROWS, DL)
            probed = dot(hidden, dp[f]).reshape(CHIPS, 2, ROWS, DL)
            outs[q, f] = jnp.concatenate(
                [straight[:, 0], hidden_factor * probed[:, 0] + straight[:, 1]], axis=1
            ).astype(BF16)
        for k, other in enumerate(reps):
            copy = remote(
                outs.at[q, other % 2, other // 2], outs_in.at[q, k], rep_s.at[q, k], rep_r.at[q, k], (other, zero)
            )
            copy.start()
            rep_copies[q, k] = copy

    group = rep // 2
    half = rep % 2
    repag_copies = {}
    for q in range(CHUNKS):
        total = outs[q, half, group].astype(F32)
        for k in range(len(reps)):
            rep_copies[q, k].wait_recv()
            total += outs_in[q, k].astype(F32)
        row = pl.multiple_of(q * 64 + (group // 2) * 16, 16)
        own_tokens = tok[pl.ds(pl.multiple_of(core * 128 + row, 16), 16), :].astype(F32)
        sib_tokens = tok_sib[pl.ds(row, 16), :].astype(F32)
        chosen = jnp.where(half == 0, own_tokens, sib_tokens)
        chosen = jnp.where(group % 2 == 0, chosen[0:8], chosen[8:16])
        back[q, half, group] = jnp.concatenate(
            [factor * (chosen + total[0:8]), factor * total[8:16]], axis=0
        ).astype(BF16)
        for k, other in enumerate(reps):
            copy = remote(
                back.at[q, half, group], back.at[q, half, group], repag_s.at[q, k], repag_r.at[q, k], (other, zero)
            )
            copy.start()
            repag_copies[q, k] = copy

    ys_copies = []
    rs2_copies = {}
    for q in range(CHUNKS):
        for k in range(len(reps)):
            repag_copies[q, k].wait_recv()
        copy = remote(back.at[q, 1], y_ref.at[core, q], ys_s.at[q], ys_r.at[q], sibling)
        copy.start()
        ys_copies.append(copy)
        signals = [back[q, f].reshape(CHIPS * 16, DL) for f in range(2)]
        straight = (dot_last(signals[0], dm[0]) + dot_last(signals[1], dm[1])).reshape(CHIPS, 2, ROWS, HL)
        probed = (dot_last(signals[0], dp[0]) + dot_last(signals[1], dp[1])).reshape(CHIPS, 2, ROWS, HL)
        both = jnp.concatenate([straight[:, 0], straight[:, 1] + hidden_factor * probed[:, 0]], axis=1)
        hid_own[...] = both
        hid[q] = both.astype(BF16)
        for k, other in enumerate(chips):
            copy = remote(hid.at[q, other], hid_in.at[q, k], rs2_s.at[q, k], rs2_r.at[q, k], (rep, other * 2 + core))
            copy.start()
            rs2_copies[q, k] = copy
        y_ref[core, q] = back[q, 0]

    ag4_copies = {}
    forwards = []
    for q in range(CHUNKS):
        total = hid[q, chip].astype(F32)
        for k in range(len(chips)):
            rs2_copies[q, k].wait_recv()
            total += hid_in[q, k].astype(F32)
        signal, signal_tan = total[0:8], total[8:16]
        gate_back = signal * mult[q, 0]
        up_back = signal * mult[q, 1]
        gate_back_tan = signal_tan * mult[q, 0] + signal * mult[q, 2]
        up_back_tan = signal_tan * mult[q, 1] + signal * mult[q, 3]
        g_ref[core, q, chip] = jnp.concatenate([gate_back, up_back, gate_back_tan, up_back_tan], axis=0).astype(BF16)
        for k, other in enumerate(chips):
            copy = remote(
                g_ref.at[core, q, chip], g_ref.at[core, q, chip], ag4_s.at[q, k], ag4_r.at[q, k],
                (rep, other * 2 + core),
            )
            copy.start()
            ag4_copies[q, k] = copy
        copy = remote(
            g_ref.at[core, q, chip], g_ref.at[core, q, chip], fw_s.at[q, 7], fw_r.at[q, 7], sibling
        )
        copy.start()
        forwards.append(copy)
    for q in range(CHUNKS):
        for k, origin in enumerate(chips_from):
            ag4_copies[q, k].wait_recv()
            copy = remote(
                g_ref.at[core, q, origin], g_ref.at[core, q, origin], fw_s.at[q, k], fw_r.at[q, k], sibling
            )
            copy.start()
            forwards.append(copy)

    for copies in (sib_copies, rs_copies, ag_copies, rep_copies, repag_copies, rs2_copies, ag4_copies):
        for copy in copies.values():
            copy.wait_send()
    for copy in pre_copies:
        copy.wait_send()
    for copies in (xs_copies, ys_copies, forwards):
        for copy in copies:
            copy.wait()


def exchange(*operands):
    vmem = pl.BlockSpec(memory_space=pltpu.VMEM)
    hbm = pl.BlockSpec(memory_space=pl.ANY)
    dma = pltpu.SemaphoreType.DMA
    peers, others = len(ZERO_STEPS), len(REP_STEPS)
    return pl.pallas_call(
        exchange_kernel,
        out_shape=(
            jax.ShapeDtypeStruct((2, CHUNKS, CHIPS, 32, HL), BF16),
            jax.ShapeDtypeStruct((2, CHUNKS, CHIPS, 16, HL), BF16),
            jax.ShapeDtypeStruct((2, CHUNKS, CHIPS, 16, DL), BF16),
        ),
        in_specs=[hbm] * 7 + [vmem] * 3,
        out_specs=(vmem, vmem, vmem),
        scratch_shapes=[
            pltpu.VMEM((256, DL), BF16),
            pltpu.VMEM((128, DL), BF16),
            pltpu.VMEM((256, DL), BF16),
            pltpu.VMEM((DL, HL), BF16),
            pltpu.VMEM((DL, HL), BF16),
            pltpu.VMEM((DL, HL), BF16),
            pltpu.VMEM((DL, HL), BF16),
            pltpu.VMEM((HL, DL), BF16),
            pltpu.VMEM((2, HL, DL), BF16),
            pltpu.VMEM((2, HL, DL), BF16),
            pltpu.VMEM((CHUNKS, 2, CHIPS, 16, HL), BF16),
            pltpu.VMEM((CHUNKS, 2, CHIPS, 16, HL), BF16),
            pltpu.VMEM((4, 128, HL), F32),
            pltpu.VMEM((CHUNKS, CHIPS, 32, HL), BF16),
            pltpu.VMEM((CHUNKS, peers, 32, HL), BF16),
            pltpu.VMEM((CHUNKS, 4, ROWS, HL), F32),
            pltpu.VMEM((CHUNKS, 2, CHIPS, 16, DL), BF16),
            pltpu.VMEM((CHUNKS, others, 16, DL), BF16),
            pltpu.VMEM((CHUNKS, 2, CHIPS, 16, DL), BF16),
            pltpu.VMEM((CHUNKS, CHIPS, 16, HL), BF16),
            pltpu.VMEM((CHIPS, 16, HL), F32),
            pltpu.VMEM((CHUNKS, peers, 16, HL), BF16),
            dma((7,)),
            dma((3,)), dma((3,)),
            dma((CHUNKS, 2)), dma((CHUNKS, 2)),
            dma((CHUNKS, peers)), dma((CHUNKS, peers)),
            dma((CHUNKS, peers)), dma((CHUNKS, peers)),
            dma((CHUNKS,)), dma((CHUNKS,)),
            dma((CHUNKS, others)), dma((CHUNKS, others)),
            dma((CHUNKS, others)), dma((CHUNKS, others)),
            dma((CHUNKS,)), dma((CHUNKS,)),
            dma((CHUNKS, peers)), dma((CHUNKS, peers)),
            dma((CHUNKS, peers)), dma((CHUNKS, peers)),
            dma((CHUNKS, peers + 1)), dma((CHUNKS, peers + 1)),
        ],
        compiler_params=pltpu.CompilerParams(
            collective_id=0, has_side_effects=True, vmem_limit_bytes=48 * 2**20
        ),
        name="exchange",
    )(*operands)


def products_kernel(tok, g, x, y, gg, ug, dg, gh, uh, dh, square, wide, sems):
    hidden = x[...].reshape(512, HL)
    signals = y[...].astype(F32).reshape(32, 2, ROWS, DL)
    straight = jnp.concatenate([signals[:, 0], jnp.zeros_like(signals[:, 0])], axis=1)
    swapped = jnp.concatenate([signals[:, 1], signals[:, 0]], axis=1)
    copies = []

    def put(buffer, n, out, sem):
        copy = pltpu.make_async_copy(buffer.at[n], out, sems.at[sem])
        copy.start()
        copies.append(copy)

    wide[0] = dot_rows(hidden, straight.astype(BF16).reshape(512, DL))
    put(wide, 0, dg, 0)
    wide[1] = dot_rows(hidden, swapped.astype(BF16).reshape(512, DL))
    put(wide, 1, dh, 1)
    tokens = tok[...]
    for n, out in enumerate((gg, ug, gh, uh)):
        part = g[:, :, :, (n // 2) * 16 : (n // 2) * 16 + 16, :].astype(F32).reshape(32, 2, ROWS, HL)
        rows = part[:, n % 2].reshape(256, HL).astype(BF16)
        square[n] = dot_rows(tokens, rows)
        put(square, n, out, 2 + n)
    for copy in copies:
        copy.wait()


def products(tok, g, x, y):
    vmem = pl.BlockSpec(memory_space=pltpu.VMEM)
    hbm = pl.BlockSpec(memory_space=pl.ANY)
    tall = jax.ShapeDtypeStruct((DL, HL), F32)
    flat = jax.ShapeDtypeStruct((HL, DL), F32)
    return pl.pallas_call(
        products_kernel,
        out_shape=(tall, tall, flat, tall, tall, flat),
        in_specs=[vmem] * 4,
        out_specs=[hbm] * 6,
        scratch_shapes=[
            pltpu.VMEM((4, DL, HL), F32),
            pltpu.VMEM((2, HL, DL), F32),
            pltpu.SemaphoreType.DMA((6,)),
        ],
        compiler_params=pltpu.CompilerParams(vmem_limit_bytes=48 * 2**20),
        name="products",
    )(tok, g, x, y)


def local(
    tokens, gate_weight, up_weight, down_weight, gate_scale, up_scale, down_scale, gate_probe, up_probe, down_probe
):
    g, x, y = exchange(
        tokens, gate_weight, up_weight, down_weight, gate_probe, up_probe, down_probe,
        gate_scale.reshape(1, DL), up_scale.reshape(1, DL), down_scale.reshape(1, HL),
    )
    return products(tokens, g, x, y)


def solution(mesh):
    in_specs = (
        P(None, "zero"),
        P("zero", "rep"),
        P("zero", "rep"),
        P("rep", "zero"),
        P("zero"),
        P("zero"),
        P("rep"),
        P("zero", "rep"),
        P("zero", "rep"),
        P("rep", "zero"),
    )
    out_specs = (
        P("zero", "rep"),
        P("zero", "rep"),
        P("rep", "zero"),
        P("zero", "rep"),
        P("zero", "rep"),
        P("rep", "zero"),
    )
    return jax.shard_map(local, mesh=mesh, in_specs=in_specs, out_specs=out_specs, check_vma=False)
```

time: 477 us -> 88.1 us (0.18)
  waiting for transfers between devices: 427 us -> 0 us
  Pallas kernels: 0 us -> 75.9 us
  matrix products: 17.7 us -> 0 us
  between operations: 13.9 us -> 0.66 us
  other arithmetic: 6.83 us -> 0 us
    psum x3 -> x0, waiting for transfers between devices: 427 us -> none  [the longest x1 159 us: local(): output, output_tan = lax.psum((output_part, output_tan_part), 'rep')]
    pallas_call x0 -> x2, Pallas kernels: none -> 75.9 us  [the longest x1 71.8 us: exchange(): pl.pallas_call(exchange_kernel, out_shape=(jax.ShapeDtypeStruct((2, CHUNK...]
    dot_general x14 -> x0, matrix products: 17.7 us -> none  [the longest x7 10 us: matmul(): return jnp.dot(left, right, preferred_element_type=jnp.float32)]
    convert_element_type x3 -> x0, other arithmetic: 6.83 us -> none  [the longest x1 3.27 us: local(): gate_back_tan = (hid_back_tan * up_pre * slope + hid_back * (up_tan * slo...]
  transfers between devices with their start and end apart: 3 -> 0, of which waited for: 3 -> 0; matrix products, arithmetic and copies ran while one was open for 1% -> 0% of each run, Pallas kernels for 0% -> 0%
where the time goes in v1:
time: 88.1 us; the launch traced here: 87.6 us
  Pallas kernels  75.9 us (86%)
  local copies, waits for them, and re-layouts  11.1 us (13%)
    pallas_call x1, Pallas kernels, exchange(): pl.pallas_call(exchange_kernel, out_shape=(jax.ShapeDtypeStruct((2, CHUNK...  71.8 us
    unnamed x16, local copies, waits for them, and re-layouts  9.01 us
    pallas_call x1, Pallas kernels, products(): pl.pallas_call(products_kernel, out_shape=(tall, tall, flat, tall, tall,...  4.04 us

profile of v1, /device:TPU:1, one launch (start us, length us, event | category | flops | bytes accessed | tf_op | source)
XLA Modules:
  0.0 87.6 jit_solution(11639635789501704103)
XLA Ops:
  0.6 0.7 reshape.21.gs_ref
  1.3 0.7 reshape.22.us_ref
  2.0 0.7 reshape.23.ds_ref
  2.7 0.0 copy-start.1
  2.7 0.9 %copy-done.1 = bf16[256,384]{1,0:T(8,128)(2,1)S(1)} copy-done((bf16[256,384]{1,0:T(8,128)(2,1)S(1)}, bf16[256,384]{1,0:T(8,128)(2,1)}, u32[]{:S(2)}) %copy-start.1) | copy-done | bytes 196632
  3.6 0.0 copy-start.2
  3.6 1.1 %copy-done.2 = bf16[384,896]{1,0:T(8,128)(2,1)S(1)} copy-done((bf16[384,896]{1,0:T(8,128)(2,1)S(1)}, bf16[384,896]{1,0:T(8,128)(2,1)}, u32[]{:S(2)}) %copy-start.2) | copy-done | bytes 688152
  4.7 0.0 copy-start.3
  4.7 1.1 %copy-done.3 = bf16[384,896]{1,0:T(8,128)(2,1)S(1)} copy-done((bf16[384,896]{1,0:T(8,128)(2,1)S(1)}, bf16[384,896]{1,0:T(8,128)(2,1)}, u32[]{:S(2)}) %copy-start.3) | copy-done | bytes 688152
  5.8 0.0 copy-start.4
  5.8 1.1 %copy-done.4 = bf16[896,384]{1,0:T(8,128)(2,1)S(1)} copy-done((bf16[896,384]{1,0:T(8,128)(2,1)S(1)}, bf16[896,384]{1,0:T(8,128)(2,1)}, u32[]{:S(2)}) %copy-start.4) | copy-done | bytes 688152
  6.9 0.0 copy-start.5
  6.9 1.1 %copy-done.5 = bf16[384,896]{1,0:T(8,128)(2,1)S(1)} copy-done((bf16[384,896]{1,0:T(8,128)(2,1)S(1)}, bf16[384,896]{1,0:T(8,128)(2,1)}, u32[]{:S(2)}) %copy-start.5) | copy-done | bytes 688152
  8.0 0.0 copy-start.6
  8.0 1.1 %copy-done.6 = bf16[384,896]{1,0:T(8,128)(2,1)S(1)} copy-done((bf16[384,896]{1,0:T(8,128)(2,1)S(1)}, bf16[384,896]{1,0:T(8,128)(2,1)}, u32[]{:S(2)}) %copy-start.6) | copy-done | bytes 688152
  9.1 0.0 copy-start.7
  9.1 1.1 %copy-done.7 = bf16[896,384]{1,0:T(8,128)(2,1)S(1)} copy-done((bf16[896,384]{1,0:T(8,128)(2,1)S(1)}, bf16[896,384]{1,0:T(8,128)(2,1)}, u32[]{:S(2)}) %copy-start.7) | copy-done | bytes 688152
  10.2 71.8 %exchange.1 = (bf16[2,2,8,32,896]{4,3,2,1,0:T(8,128)(2,1)}, bf16[2,2,8,16,896]{4,3,2,1,0:T(8,128)(2,1)S(1)}, bf16[2,2,8,16,384]{4,3,2,1,0:T(8,128)(2,1)S(1)}) custom-call(bf16[256,384]{1,0:T(8,128)(2,1)S(1)} %copy-done.1, bf16[384,896]{1,0:T(8,128)(2,1)S(1)} %copy-done.2, bf16[384,896]{1,0:T(8,128)(2,1)S(1)} %copy-done.3, bf16[896,384]{1,0:T(8,128)(2,1)S(1)} %copy-done.4, ...), custom_call_target="tpu_custom_call" | custom-call | tf_op jit(solution)/shard_map/exchange/pallas_call | solution.py:309
  82.0 0.0 copy-start
  82.1 1.5 %copy-done = bf16[2,2,8,32,896]{4,3,2,1,0:T(8,128)(2,1)S(1)} copy-done((bf16[2,2,8,32,896]{4,3,2,1,0:T(8,128)(2,1)S(1)}, bf16[2,2,8,32,896]{4,3,2,1,0:T(8,128)(2,1)}, u32[]{:S(2)}) %copy-start) | copy-done | bytes 1835032
  83.5 4.0 %products.1 = (f32[384,896]{1,0:T(8,128)}, f32[384,896]{1,0:T(8,128)}, f32[896,384]{1,0:T(8,128)}, f32[384,896]{1,0:T(8,128)}, f32[384,896]{1,0:T(8,128)}, /*index=5*/f32[896,384]{1,0:T(8,128)}) custom-call(bf16[256,384]{1,0:T(8,128)(2,1)S(1)} %copy-done.1, bf16[2,2,8,32,896]{4,3,2,1,0:T(8,128)(2,1)S(1)} %copy-done, ...), custom_call_target="tpu_custom_call" | custom-call | tf_op jit(solution)/shard_map/products/pallas_call | solution.py:392
Async XLA Ops:
  2.7 0.9 %copy-start.1 = (bf16[256,384]{1,0:T(8,128)(2,1)S(1)}, bf16[256,384]{1,0:T(8,128)(2,1)}, u32[]{:S(2)}) copy-start(bf16[256,384]{1,0:T(8,128)(2,1)} %tok.1) | copy-start | bytes 589828
  3.6 1.1 %copy-start.2 = (bf16[384,896]{1,0:T(8,128)(2,1)S(1)}, bf16[384,896]{1,0:T(8,128)(2,1)}, u32[]{:S(2)}) copy-start(bf16[384,896]{1,0:T(8,128)(2,1)} %gw_hbm.1) | copy-start | bytes 2064388
  4.7 1.1 %copy-start.3 = (bf16[384,896]{1,0:T(8,128)(2,1)S(1)}, bf16[384,896]{1,0:T(8,128)(2,1)}, u32[]{:S(2)}) copy-start(bf16[384,896]{1,0:T(8,128)(2,1)} %uw_hbm.1) | copy-start | bytes 2064388
  5.8 1.1 %copy-start.4 = (bf16[896,384]{1,0:T(8,128)(2,1)S(1)}, bf16[896,384]{1,0:T(8,128)(2,1)}, u32[]{:S(2)}) copy-start(bf16[896,384]{1,0:T(8,128)(2,1)} %dw_hbm.1) | copy-start | bytes 2064388
  6.9 1.1 %copy-start.5 = (bf16[384,896]{1,0:T(8,128)(2,1)S(1)}, bf16[384,896]{1,0:T(8,128)(2,1)}, u32[]{:S(2)}) copy-start(bf16[384,896]{1,0:T(8,128)(2,1)} %gp_hbm.1) | copy-start | bytes 2064388
  8.0 1.1 %copy-start.6 = (bf16[384,896]{1,0:T(8,128)(2,1)S(1)}, bf16[384,896]{1,0:T(8,128)(2,1)}, u32[]{:S(2)}) copy-start(bf16[384,896]{1,0:T(8,128)(2,1)} %up_hbm.1) | copy-start | bytes 2064388
  9.1 1.1 %copy-start.7 = (bf16[896,384]{1,0:T(8,128)(2,1)S(1)}, bf16[896,384]{1,0:T(8,128)(2,1)}, u32[]{:S(2)}) copy-start(bf16[896,384]{1,0:T(8,128)(2,1)} %dp_hbm.1) | copy-start | bytes 2064388
  82.0 1.5 %copy-start = (bf16[2,2,8,32,896]{4,3,2,1,0:T(8,128)(2,1)S(1)}, bf16[2,2,8,32,896]{4,3,2,1,0:T(8,128)(2,1)}, u32[]{:S(2)}) copy-start(bf16[2,2,8,32,896]{4,3,2,1,0:T(8,128)(2,1)} %get-tuple-element.9.g) | copy-start | bytes 5505028

commit v2 on v0

v2 whole, which is shorter than its diff:
```python
import functools

import jax
import jax.numpy as jnp
from jax import lax
from jax.experimental import pallas as pl
from jax.experimental.pallas import tpu as pltpu
from jax.sharding import PartitionSpec as P

D = 6144
H = 14336
TOKENS = 256

DL = 384
HL = 896
CHUNKS = 2
GROUPS = 8
ROWS = 8
BG = (1, 1, 0)
COPIES = 128

BF16 = jnp.bfloat16
F32 = jnp.float32
MESH = pl.DeviceIdType.MESH

ZERO_STEPS = ((1, 2), (1, 1), (1, 3), (0, 2), (1, 0), (0, 1), (0, 3))
RING_STEPS = (2, 1, 3)


def dot(left, right):
    return jnp.dot(left, right, preferred_element_type=F32)


def dot_last(left, right):
    return lax.dot_general(left, right, (((1,), (1,)), ((), ())), preferred_element_type=F32)


def dot_rows(left, right):
    return lax.dot_general(left, right, (((0,), (0,)), ((), ())), preferred_element_type=F32)


def pair(first, second):
    width = first.shape[-1]
    return jnp.concatenate([first.reshape(-1, ROWS, width), second.reshape(-1, ROWS, width)], axis=1).astype(BF16)


class Copies:
    def __init__(self, send, recv):
        self.send, self.recv = send, recv
        self.open = []

    def start(self, src, dst, device):
        n = len(self.open)
        copy = pltpu.make_async_remote_copy(
            src_ref=src, dst_ref=dst, send_sem=self.send.at[n], recv_sem=self.recv.at[n],
            device_id=device, device_id_type=MESH,
        )
        copy.start()
        entry = [copy, True]
        self.open.append(entry)
        return entry

    def arrive(self, *entries):
        for entry in entries:
            entry[0].wait_recv()
            entry[1] = False

    def finish(self):
        for copy, coming in self.open:
            copy.wait_send()
            if coming:
                copy.wait_recv()


def exchange_kernel(
    tok_hbm, gw_hbm, uw_hbm, dw_hbm, gp_hbm, up_hbm, dp_hbm, gs_hbm, us_hbm, ds_hbm,
    g_ref, dg_ref, dh_ref, turned,
    tok, tok_sib, tok_order, gw, uw, gp, up, dw, dm, dp, gs, us, ds,
    sib_out, sib_in, own, stage, far4, near4, sum4, mine4,
    x_ref, y_ref, hids, mult, outs, outs_in, mids, mids_in, back,
    hid, hid_in,
    load_sem, send_sem, recv_sem,
):
    rep = lax.axis_index("rep")
    zero = lax.axis_index("zero")
    core = zero % 2
    z_lo, x = zero // 8, (zero // 2) % 4
    z_hi, y = rep // 4, rep % 4
    sibling = (rep, zero + 1 - 2 * core)
    twin = (rep, (1 - z_lo) * 8 + x * 2 + core)
    xs = [(x + step) % 4 for step in RING_STEPS]
    ys = [(y + step) % 4 for step in RING_STEPS]
    zs = [(z_hi + step) % 4 for step in RING_STEPS]
    x_peers = [(rep, z_lo * 8 + other * 2 + core) for other in xs]
    y_peers = [(z_hi * 4 + other, zero) for other in ys]
    z_peers = [(other * 4 + y, zero) for other in zs]
    chips = [((x + dx) % 4, (z_lo + dz) % 2) for dz, dx in ZERO_STEPS]
    chips_from = [((x + 4 - dx) % 4, (z_lo + dz) % 2) for dz, dx in ZERO_STEPS]
    chip_peers = [(rep, other_z * 8 + other_x * 2 + core) for other_x, other_z in chips]
    partners = [sibling] + chip_peers + y_peers + z_peers
    copies = Copies(send_sem, recv_sem)

    barrier = pltpu.get_barrier_semaphore()
    for other in partners:
        pl.semaphore_signal(barrier, inc=1, device_id=other, device_id_type=MESH)

    pairs = (
        (tok_hbm, tok), (gp_hbm, gp), (up_hbm, up), (gs_hbm, gs), (gw_hbm, gw), (us_hbm, us), (uw_hbm, uw),
        (ds_hbm, ds), (dw_hbm, dw), (dp_hbm, dp.at[0]),
    )
    loads = [pltpu.make_async_copy(src, dst, load_sem.at[n]) for n, (src, dst) in enumerate(pairs)]
    for copy in loads:
        copy.start()

    loads[0].wait()
    tok_order[0:128, :] = tok[pl.ds(pl.multiple_of((1 - core) * 128, 128), 128), :]
    tok_order[128:256, :] = tok[pl.ds(pl.multiple_of(core * 128, 128), 128), :]
    tokens = tok_order[...]

    def scaled(ref, scale_ref, out_ref):
        rows, width = ref.shape
        column = jnp.broadcast_to(scale_ref[...].reshape(1, rows), (128, rows)).T
        for n in range(width // 128):
            block = slice(n * 128, (n + 1) * 128)
            out_ref[:, block] = (ref[:, block].astype(F32) * column).astype(BF16)

    from_sib = {}

    def pre(p, first, second):
        a = dot(tokens, first)
        b = dot(tokens, second)
        own[2 * p] = a[128:256]
        own[2 * p + 1] = b[128:256]
        both = pair(a[0:128], b[0:128])
        for q in range(CHUNKS):
            sib_out[q, p] = both[q * GROUPS : (q + 1) * GROUPS]

    def send_pre(p):
        for q in range(CHUNKS):
            from_sib[q, p] = copies.start(sib_out.at[q, p], sib_in.at[q, p], sibling)

    def sum_start(q, parts, far, near):
        if q == 0:
            return [copies.start(parts.at[other], far.at[k], x_peers[k]) for k, other in enumerate(xs)]
        return [copies.start(parts.at[:, 1 - z_lo], near, twin)]

    def sum_middle(q, parts, far, near, out, mine, ours, arrivals):
        if q == 0:
            total = ours
            for k, entry in enumerate(arrivals):
                copies.arrive(entry)
                total = total + far[k].astype(F32)
            mine[...] = jnp.where(z_lo == 0, total[0], total[1])
            out[0] = jnp.where(z_lo == 0, total[1], total[0]).astype(BF16)
            return [copies.start(out.at[0], near.at[0], twin)]
        copies.arrive(*arrivals)
        out[...] = (parts[:, z_lo].astype(F32) + near[...].astype(F32)).astype(BF16)
        entries = [copies.start(out.at[other], far.at[k, 0], x_peers[k]) for k, other in enumerate(xs)]
        mine[...] = ours + near[x].astype(F32)
        return entries

    def sum_end(q, far, near, mine, arrivals):
        copies.arrive(*arrivals)
        total = mine[...]
        if q == 0:
            return total + near[0].astype(F32)
        for k in range(3):
            total = total + far[k, 0].astype(F32)
        return total

    def gather(blocks):
        block = blocks.at[x, z_lo]
        return [copies.start(block, block, peer) for peer in chip_peers]

    feature_factor = float(D) ** -0.5
    hidden_factor = float(H) ** -0.5
    factor = float(TOKENS) ** -0.5

    def start_first(q):
        for p in range(2):
            copies.arrive(from_sib[q, p])
            a = own[2 * p, q * 64 : (q + 1) * 64].reshape(GROUPS, ROWS, HL)
            b = own[2 * p + 1, q * 64 : (q + 1) * 64].reshape(GROUPS, ROWS, HL)
            both = (jnp.concatenate([a, b], axis=1) + sib_in[q, p].astype(F32)).astype(BF16)
            stage[q, :, :, p * 16 : (p + 1) * 16, :] = both.reshape(4, 2, 16, HL)
        return sum_start(q, stage.at[q], far4.at[q], near4.at[q])

    def middle_first(q, arrivals):
        count = 2 if q == 0 else 1
        group = x * 2 if q == 0 else x * 2 + z_lo
        rows = pl.ds(pl.multiple_of(q * 64 + group * ROWS, ROWS), count * ROWS)
        kept = [own[n, rows, :].reshape(count, ROWS, HL) for n in range(4)]
        theirs = [sib_in[q, p, pl.ds(group, count)].astype(F32) for p in range(2)]
        ours = jnp.concatenate(kept, axis=1) + jnp.concatenate(theirs, axis=1)
        if q == 1:
            ours = ours[0]
        return sum_middle(q, stage.at[q], far4.at[q], near4.at[q], sum4.at[q], mine4.at[q], ours, arrivals)

    multipliers = []

    def activate(q, arrivals):
        total = sum_end(q, far4.at[q], near4.at[q], mine4.at[q], arrivals)
        gate_tan, up_tan, gate_pre, up_pre = [total[n * ROWS : (n + 1) * ROWS] for n in range(4)]
        gate_tan = feature_factor * gate_tan
        up_tan = feature_factor * up_tan
        logistic = jax.nn.sigmoid(gate_pre)
        act = gate_pre * logistic
        slope = logistic * (1.0 + gate_pre * (1.0 - logistic))
        bend = logistic * (1.0 - logistic) * (2.0 + gate_pre * (1.0 - 2.0 * logistic))
        lean = slope * gate_tan
        x_ref[core, q, x, z_lo] = jnp.concatenate([act * up_pre, lean * up_pre + act * up_tan], axis=0).astype(BF16)
        entries = gather(x_ref.at[core, q])
        mult[core, q, x, z_lo] = jnp.concatenate(
            [up_pre * slope, act, up_tan * slope + up_pre * bend * gate_tan, lean], axis=0
        ).astype(BF16)
        block = mult.at[core, q, x, z_lo]
        multipliers.append([copies.start(block, block, twin)])
        return entries

    waiting = list(range(CHUNKS))

    def background(count):
        for q in waiting[:count]:
            copies.arrive(*multipliers[q])
            block = mult.at[core, q, x]
            multipliers[q] = [copies.start(block, block, peer) for peer in x_peers]
        del waiting[:count]

    def share_multipliers(q):
        copies.arrive(*multipliers[q])
        return copies.start(mult.at[core, q], mult.at[core, q], sibling)

    def output(q, arrivals):
        copies.arrive(*arrivals)
        hidden = x_ref[core, q].reshape(GROUPS * 16, HL)
        for f in range(2):
            straight = dot(hidden, dm[f]).reshape(GROUPS, 2, ROWS, DL)
            probed = dot(hidden, dp[f]).reshape(GROUPS, 2, ROWS, DL)
            outs[q, f] = jnp.concatenate(
                [straight[:, 0], hidden_factor * probed[:, 0] + straight[:, 1]], axis=1
            ).astype(BF16).reshape(2, 4, 16, DL)
        entries = [
            copies.start(outs.at[q, other % 2, other // 2], outs_in.at[q, k], y_peers[k]) for k, other in enumerate(ys)
        ]
        return entries, copies.start(x_ref.at[core, q], x_ref.at[core, q], sibling)

    half, high = y % 2, y // 2

    def middle(q, arrivals):
        total = outs[q, half, high].astype(F32)
        for k, entry in enumerate(arrivals):
            copies.arrive(entry)
            total += outs_in[q, k].astype(F32)
        mids[q] = total.astype(BF16)
        return [copies.start(mids.at[q, other], mids_in.at[q, k], z_peers[k]) for k, other in enumerate(zs)]

    def cotangent(q, arrivals):
        total = mids[q, z_hi].astype(F32)
        for k, entry in enumerate(arrivals):
            copies.arrive(entry)
            total += mids_in[q, k].astype(F32)
        row = pl.multiple_of(q * 64 + high * 32 + (z_hi // 2) * 16, 16)
        own_tokens = tok[pl.ds(pl.multiple_of(core * 128 + row, 16), 16), :].astype(F32)
        sib_tokens = tok_sib[pl.ds(row, 16), :].astype(F32)
        chosen = jnp.where(half == 0, own_tokens, sib_tokens)
        chosen = jnp.where(z_hi % 2 == 0, chosen[0:8], chosen[8:16])
        back[q, half, high, z_hi] = jnp.concatenate(
            [factor * (chosen + total[0:8]), factor * total[8:16]], axis=0
        ).astype(BF16)
        block = back.at[q, half, high, z_hi]
        return [copies.start(block, block, peer) for peer in z_peers]

    def spread(q, arrivals):
        copies.arrive(*arrivals)
        block = back.at[q, half, high]
        return [copies.start(block, block, peer) for peer in y_peers]

    def backward(q, arrivals):
        copies.arrive(*arrivals)
        signals = [back[q, f].reshape(GROUPS * 16, DL) for f in range(2)]
        straight = (dot_last(signals[0], dm[0]) + dot_last(signals[1], dm[1])).reshape(GROUPS, 2, ROWS, HL)
        probed = (dot_last(signals[0], dp[0]) + dot_last(signals[1], dp[1])).reshape(GROUPS, 2, ROWS, HL)
        both = jnp.concatenate([straight[:, 0], straight[:, 1] + hidden_factor * probed[:, 0]], axis=1)
        hid[q] = both.astype(BF16).reshape(4, 2, 16, HL)
        entries = [copies.start(hid.at[q, *chip], hid_in.at[q, k], chip_peers[k]) for k, chip in enumerate(chips)]
        shared = copies.start(back.at[q, 1], y_ref.at[core, q], sibling)
        y_ref[core, q] = back[q, 0]
        return entries, shared

    def gradients(q, arrivals):
        total = hid[q, x, z_lo].astype(F32)
        for k, entry in enumerate(arrivals):
            copies.arrive(entry)
            total += hid_in[q, k].astype(F32)
        hids[core, q, x, z_lo] = total.astype(BF16)
        entries = gather(hids.at[core, q])
        block = hids.at[core, q, x, z_lo]
        return entries, copies.start(block, block, sibling)

    def combine(side, q, place_x, place_z):
        signals = hids[side, q, place_x, place_z].astype(F32)
        signal, signal_tan = signals[0:8], signals[8:16]
        factors = mult[side, q, place_x, place_z].astype(F32)
        first, second, third, fourth = [factors[n * ROWS : (n + 1) * ROWS] for n in range(4)]
        g_ref[side, q, place_x, place_z] = jnp.concatenate(
            [
                signal * first,
                signal * second,
                signal_tan * first + signal * third,
                signal_tan * second + signal * fourth,
            ],
            axis=0,
        ).astype(BF16)

    def down_products():
        hidden = x_ref[...].reshape(512, HL)
        signals = y_ref[...].astype(F32).reshape(32, 2, ROWS, DL)
        straight = jnp.concatenate([signals[:, 0], jnp.zeros_like(signals[:, 0])], axis=1)
        swapped = jnp.concatenate([signals[:, 1], signals[:, 0]], axis=1)
        dg_ref[...] = dot_rows(hidden, straight.astype(BF16).reshape(512, DL))
        dh_ref[...] = dot_rows(hidden, swapped.astype(BF16).reshape(512, DL))

    def prefetch():
        loads[7].wait()
        loads[8].wait()
        scaled(dw, ds, dm.at[0])
        loads[9].wait()
        theirs = tok.at[pl.ds(pl.multiple_of((1 - core) * 128, 128), 128)]
        return [
            copies.start(dm.at[0], dm.at[1], sibling),
            copies.start(dp.at[0], dp.at[1], sibling),
            copies.start(theirs, tok_sib, sibling),
        ]

    chunks = range(CHUNKS)
    loads[1].wait()
    loads[2].wait()
    pre(0, gp[...], up[...])
    pl.semaphore_wait(barrier, len(partners))
    send_pre(0)
    loads[3].wait()
    loads[4].wait()
    scaled(gw, gs, gw)
    loads[5].wait()
    loads[6].wait()
    scaled(uw, us, uw)
    pre(1, gw[...], uw[...])
    send_pre(1)
    flying = [start_first(q) for q in chunks]
    prefetched = prefetch()
    flying = [middle_first(q, flying[q]) for q in chunks]
    flying = [activate(q, flying[q]) for q in chunks]
    copies.arrive(*prefetched)
    shared = []
    flying, kept = zip(*[output(q, flying[q]) for q in chunks])
    shared += kept
    background(BG[0])
    turned[...] = tok[...].astype(F32).T.astype(BF16)
    flying = [middle(q, flying[q]) for q in chunks]
    background(BG[1])
    flying = [cotangent(q, flying[q]) for q in chunks]
    background(BG[2])
    flying = [spread(q, flying[q]) for q in chunks]
    flying, kept = zip(*[backward(q, flying[q]) for q in chunks])
    shared += kept
    shared += [share_multipliers(q) for q in chunks]
    flying, first = zip(*[gradients(q, flying[q]) for q in chunks])
    copies.arrive(*shared)
    for q in chunks:
        combine(core, q, x, z_lo)
    down_products()
    order = list(reversed(range(len(chips))))
    passed = []
    for q in chunks:
        for k in order:
            copies.arrive(flying[q][k])
            block = hids.at[core, q, *chips_from[k]]
            passed.append((q, k, copies.start(block, block, sibling)))
            combine(core, q, *chips_from[k])
    for q in chunks:
        copies.arrive(first[q])
        combine(1 - core, q, x, z_lo)
    for q, k, entry in passed:
        copies.arrive(entry)
        combine(1 - core, q, *chips_from[k])
    copies.finish()


def exchange(*operands):
    vmem = pl.BlockSpec(memory_space=pltpu.VMEM)
    hbm = pl.BlockSpec(memory_space=pltpu.HBM)
    return pl.pallas_call(
        exchange_kernel,
        out_shape=(
            pltpu.VMEM((2, CHUNKS, 4, 2, 32, HL), BF16),
            pltpu.VMEM((HL, DL), F32),
            pltpu.VMEM((HL, DL), F32),
            pltpu.VMEM((DL, 256), BF16),
        ),
        in_specs=[hbm] * 10,
        out_specs=(vmem, vmem, vmem, vmem),
        scratch_shapes=[
            pltpu.VMEM((256, DL), BF16),
            pltpu.VMEM((128, DL), BF16),
            pltpu.VMEM((256, DL), BF16),
            pltpu.VMEM((DL, HL), BF16),
            pltpu.VMEM((DL, HL), BF16),
            pltpu.VMEM((DL, HL), BF16),
            pltpu.VMEM((DL, HL), BF16),
            pltpu.VMEM((HL, DL), BF16),
            pltpu.VMEM((2, HL, DL), BF16),
            pltpu.VMEM((2, HL, DL), BF16),
            pltpu.VMEM((DL,), F32),
            pltpu.VMEM((DL,), F32),
            pltpu.VMEM((HL,), F32),
            pltpu.VMEM((CHUNKS, 2, GROUPS, 16, HL), BF16),
            pltpu.VMEM((CHUNKS, 2, GROUPS, 16, HL), BF16),
            pltpu.VMEM((4, 128, HL), F32),
            pltpu.VMEM((CHUNKS, 4, 2, 32, HL), BF16),
            pltpu.VMEM((CHUNKS, 3, 2, 32, HL), BF16),
            pltpu.VMEM((CHUNKS, 4, 32, HL), BF16),
            pltpu.VMEM((CHUNKS, 4, 32, HL), BF16),
            pltpu.VMEM((CHUNKS, 32, HL), F32),
            pltpu.VMEM((2, CHUNKS, 4, 2, 16, HL), BF16),
            pltpu.VMEM((2, CHUNKS, 2, 4, 16, DL), BF16),
            pltpu.VMEM((2, CHUNKS, 4, 2, 16, HL), BF16),
            pltpu.VMEM((2, CHUNKS, 4, 2, 32, HL), BF16),
            pltpu.VMEM((CHUNKS, 2, 2, 4, 16, DL), BF16),
            pltpu.VMEM((CHUNKS, 3, 4, 16, DL), BF16),
            pltpu.VMEM((CHUNKS, 4, 16, DL), BF16),
            pltpu.VMEM((CHUNKS, 3, 16, DL), BF16),
            pltpu.VMEM((CHUNKS, 2, 2, 4, 16, DL), BF16),
            pltpu.VMEM((CHUNKS, 4, 2, 16, HL), BF16),
            pltpu.VMEM((CHUNKS, len(ZERO_STEPS), 16, HL), BF16),
            pltpu.SemaphoreType.DMA((10,)),
            pltpu.SemaphoreType.DMA((COPIES,)),
            pltpu.SemaphoreType.DMA((COPIES,)),
        ],
        compiler_params=pltpu.CompilerParams(
            collective_id=0, has_side_effects=True, vmem_limit_bytes=44 * 2**20
        ),
        name="exchange",
    )(*[pltpu.with_memory_space_constraint(operand, pltpu.HBM) for operand in operands])


def products_kernel(turned, g, down, down_tan, gg, ug, dg, gh, uh, dh, square, sems):
    copies = []

    def put(src, out, sem):
        copy = pltpu.make_async_copy(src, out, sems.at[sem])
        copy.start()
        copies.append(copy)

    put(down, dg, 0)
    put(down_tan, dh, 1)
    tokens = turned[...]
    for n, out in enumerate((gg, ug, gh, uh)):
        part = g[:, :, :, :, (n // 2) * 16 : (n // 2) * 16 + 16, :].astype(F32).reshape(32, 2, ROWS, HL)
        rows = part[:, n % 2].reshape(256, HL).astype(BF16)
        square[n] = dot(tokens, rows)
        put(square.at[n], out, 2 + n)
    for copy in copies:
        copy.wait()


def products(turned, g, down, down_tan):
    vmem = pl.BlockSpec(memory_space=pltpu.VMEM)
    hbm = pl.BlockSpec(memory_space=pl.ANY)
    tall = jax.ShapeDtypeStruct((DL, HL), F32)
    flat = jax.ShapeDtypeStruct((HL, DL), F32)
    return pl.pallas_call(
        products_kernel,
        out_shape=(tall, tall, flat, tall, tall, flat),
        in_specs=[vmem] * 4,
        out_specs=[hbm] * 6,
        scratch_shapes=[pltpu.VMEM((4, DL, HL), F32), pltpu.SemaphoreType.DMA((6,))],
        compiler_params=pltpu.CompilerParams(vmem_limit_bytes=40 * 2**20),
        name="products",
    )(turned, g, down, down_tan)


def local(
    tokens, gate_weight, up_weight, down_weight, gate_scale, up_scale, down_scale, gate_probe, up_probe, down_probe
):
    g, down, down_tan, turned = exchange(
        tokens, gate_weight, up_weight, down_weight, gate_probe, up_probe, down_probe,
        gate_scale, up_scale, down_scale,
    )
    return products(turned, g, down, down_tan)


def solution(mesh):
    in_specs = (
        P(None, "zero"),
        P("zero", "rep"),
        P("zero", "rep"),
        P("rep", "zero"),
        P("zero"),
        P("zero"),
        P("rep"),
        P("zero", "rep"),
        P("zero", "rep"),
        P("rep", "zero"),
    )
    out_specs = (
        P("zero", "rep"),
        P("zero", "rep"),
        P("rep", "zero"),
        P("zero", "rep"),
        P("zero", "rep"),
        P("rep", "zero"),
    )
    return jax.shard_map(local, mesh=mesh, in_specs=in_specs, out_specs=out_specs, check_vma=False)
```

time: 477 us -> 68.1 us (0.14)
  waiting for transfers between devices: 427 us -> 0 us
  Pallas kernels: 0 us -> 67.4 us
  matrix products: 17.7 us -> 0 us
  between operations: 13.9 us -> 0.64 us
  local copies, waits for them, and re-layouts: 11.3 us -> 0 us
  other arithmetic: 6.83 us -> 0 us
    psum x3 -> x0, waiting for transfers between devices: 427 us -> none  [the longest x1 159 us: local(): output, output_tan = lax.psum((output_part, output_tan_part), 'rep')]
    pallas_call x0 -> x2, Pallas kernels: none -> 67.4 us  [the longest x1 64 us: exchange(): pl.pallas_call(exchange_kernel, out_shape=(pltpu.VMEM((2, CHUNKS, 4, 2, 3...]
    dot_general x14 -> x0, matrix products: 17.7 us -> none  [the longest x7 10 us: matmul(): return jnp.dot(left, right, preferred_element_type=jnp.float32)]
    unnamed x26 -> x0, local copies, waits for them, and re-layouts: 9.38 us -> none
    convert_element_type x3 -> x0, other arithmetic: 6.83 us -> none  [the longest x1 3.27 us: local(): gate_back_tan = (hid_back_tan * up_pre * slope + hid_back * (up_tan * slo...]
  transfers between devices with their start and end apart: 3 -> 0, of which waited for: 3 -> 0; matrix products, arithmetic and copies ran while one was open for 1% -> 0% of each run, Pallas kernels for 0% -> 0%
where the time goes in v2:
time: 68.1 us; the launch traced here: 68 us
  Pallas kernels  67.4 us (99%)
    pallas_call x1, Pallas kernels, exchange(): pl.pallas_call(exchange_kernel, out_shape=(pltpu.VMEM((2, CHUNKS, 4, 2, 3...  64 us
    pallas_call x1, Pallas kernels, products(): pl.pallas_call(products_kernel, out_shape=(tall, tall, flat, tall, tall,...  3.37 us

profile of v2, /device:TPU:1, one launch (start us, length us, event | category | flops | bytes accessed | tf_op | source)
XLA Modules:
  0.0 68.0 jit_solution(10750138942770891222)
XLA Ops:
  0.6 64.0 %exchange.1 = (bf16[2,2,4,2,32,896]{5,4,3,2,1,0:T(8,128)(2,1)S(1)}, f32[896,384]{1,0:T(8,128)S(1)}, f32[896,384]{1,0:T(8,128)S(1)}, bf16[384,256]{1,0:T(8,128)(2,1)S(1)}) custom-call(bf16[256,384]{1,0:T(8,128)(2,1)} %tok_hbm.1, bf16[384,896]{1,0:T(8,128)(2,1)} %gw_hbm.1, bf16[384,896]{1,0:T(8,128)(2,1)} %uw_hbm.1, bf16[896,384]{1,0:T(8,128)(2,1)} %dw_hbm.1, ...), custom_call_target="tpu_custom_call" | custom-call | tf_op jit(solution)/shard_map/exchange/pallas_call | solution.py:392
  64.6 3.4 %products.1 = (f32[384,896]{1,0:T(8,128)}, f32[384,896]{1,0:T(8,128)}, f32[896,384]{1,0:T(8,128)}, f32[384,896]{1,0:T(8,128)}, f32[384,896]{1,0:T(8,128)}, /*index=5*/f32[896,384]{1,0:T(8,128)}) custom-call(bf16[384,256]{1,0:T(8,128)(2,1)S(1)} %get-tuple-element.10.turned, bf16[2,2,4,2,32,896]{5,4,3,2,1,0:T(8,128)(2,1)S(1)} %get-tuple-element.11.g, ...), custom_call_target="tpu_custom_call" | custom-call | tf_op jit(solution)/shard_map/products/pallas_call | solution.py:471

commit v3 on v2

v3 whole, which is shorter than its diff:
```python
import functools

import jax
import jax.numpy as jnp
from jax import lax
from jax.experimental import pallas as pl
from jax.experimental.pallas import tpu as pltpu
from jax.sharding import PartitionSpec as P

D = 6144
H = 14336
TOKENS = 256

DL = 384
HL = 896
CHUNKS = 2
GROUPS = 8
ROWS = 8
BACKGROUND = (1, 1, 0)
GROUPS_SENT = 45
SENDS = 12

BF16 = jnp.bfloat16
F32 = jnp.float32
MESH = pl.DeviceIdType.MESH

ZERO_STEPS = ((1, 2), (1, 1), (1, 3), (0, 2), (1, 0), (0, 1), (0, 3))
RING_STEPS = (2, 1, 3)


def dot(left, right):
    return jnp.dot(left, right, preferred_element_type=F32)


def dot_last(left, right):
    return lax.dot_general(left, right, (((1,), (1,)), ((), ())), preferred_element_type=F32)


def dot_rows(left, right):
    return lax.dot_general(left, right, (((0,), (0,)), ((), ())), preferred_element_type=F32)


def pair(first, second):
    width = first.shape[-1]
    return jnp.concatenate([first.reshape(-1, ROWS, width), second.reshape(-1, ROWS, width)], axis=1).astype(BF16)


class Copies:
    def __init__(self, send, recv, device):
        self.send, self.recv, self.device = send, recv, device
        self.groups = []
        self.busy = {}

    def start(self, moves, view):
        n = len(self.groups)
        slot = n % SENDS
        if slot in self.busy:
            self.busy.pop(slot).wait_send()
        for src, dst, device in moves:
            pltpu.make_async_remote_copy(
                src_ref=src, dst_ref=dst, send_sem=self.send.at[slot], recv_sem=self.recv.at[n],
                device_id=device, device_id_type=MESH,
            ).start()
        group = pltpu.make_async_remote_copy(
            src_ref=view, dst_ref=view, send_sem=self.send.at[slot], recv_sem=self.recv.at[n],
            device_id=self.device, device_id_type=MESH,
        )
        self.busy[slot] = group
        self.groups.append(group)
        return group

    def one(self, src, dst, device):
        return self.start([(src, dst, device)], dst)

    def arrive(self, *groups):
        for group in groups:
            group.wait_recv()

    def sent(self):
        for slot in list(self.busy):
            self.busy.pop(slot).wait_send()


def exchange_kernel(
    tok_hbm, gw_hbm, uw_hbm, dw_hbm, gp_hbm, up_hbm, dp_hbm, gs_hbm, us_hbm, ds_hbm,
    g_ref, dg_ref, dh_ref, turned,
    tok, tok_sib, tok_order, mats, dw, wide, gs, us, ds,
    sib_out, sib_in, own, stage, far4, near4, sum4, mine4,
    x_ref, y_ref, hids, mult, outs, outs_in, mids, mids_in, back,
    hid, hid_in,
    load_sem, send_sem, recv_sem,
):
    rep = lax.axis_index("rep")
    zero = lax.axis_index("zero")
    core = lax.rem(zero, 2)
    z_lo, x = lax.div(zero, 8), lax.rem(lax.div(zero, 2), 4)
    z_hi, y = lax.div(rep, 4), lax.rem(rep, 4)
    sibling = (rep, zero + 1 - 2 * core)
    twin = (rep, (1 - z_lo) * 8 + x * 2 + core)
    ring_x = [x] + [lax.rem(x + step, 4) for step in (1, 2, 3)]
    xs = [ring_x[step] for step in RING_STEPS]
    ys = [lax.rem(y + step, 4) for step in RING_STEPS]
    zs = [lax.rem(z_hi + step, 4) for step in RING_STEPS]
    x_peers = [(rep, z_lo * 8 + other * 2 + core) for other in xs]
    y_peers = [(z_hi * 4 + other, zero) for other in ys]
    z_peers = [(other * 4 + y, zero) for other in zs]
    ring_z = [z_lo, 1 - z_lo]
    chips = [(ring_x[dx], ring_z[dz]) for dz, dx in ZERO_STEPS]
    chips_from = [(ring_x[(4 - dx) % 4], ring_z[dz]) for dz, dx in ZERO_STEPS]
    places = [2 * other_x + other_z for other_x, other_z in chips]
    places_from = [2 * other_x + other_z for other_x, other_z in chips_from]
    chip_peers = [(rep, other_z * 8 + other_x * 2 + core) for other_x, other_z in chips]
    partners = [sibling] + chip_peers + y_peers + z_peers
    copies = Copies(send_sem, recv_sem, sibling)

    barrier = pltpu.get_barrier_semaphore()
    for other in partners:
        pl.semaphore_signal(barrier, inc=1, device_id=other, device_id_type=MESH)

    gp, up = mats.at[0, :, pl.ds(0, HL)], mats.at[0, :, pl.ds(HL, HL)]
    gw, uw = mats.at[1, :, pl.ds(0, HL)], mats.at[1, :, pl.ds(HL, HL)]
    pairs = (
        (tok_hbm, tok), (gp_hbm, gp), (up_hbm, up), (gs_hbm, gs), (gw_hbm, gw), (us_hbm, us), (uw_hbm, uw),
        (ds_hbm, ds), (dw_hbm, dw), (dp_hbm, wide.at[:, pl.ds(2 * DL, DL)]),
    )
    loads = [pltpu.make_async_copy(src, dst, load_sem.at[n]) for n, (src, dst) in enumerate(pairs)]
    for copy in loads:
        copy.start()

    loads[0].wait()
    tok_order[0:128, :] = tok[pl.ds(pl.multiple_of((1 - core) * 128, 128), 128), :]
    tok_order[128:256, :] = tok[pl.ds(pl.multiple_of(core * 128, 128), 128), :]
    tokens = tok_order[...]

    def scaled(ref, scale_ref, out_ref, rows, width):
        column = jnp.broadcast_to(scale_ref[...].reshape(1, rows), (128, rows)).T
        for n in range(width // 128):
            block = slice(n * 128, (n + 1) * 128)
            out_ref[:, block] = (ref[:, block].astype(F32) * column).astype(BF16)

    from_sib = {}

    def pre(p):
        wide_result = dot(tokens, mats[p])
        a, b = wide_result[:, 0:HL], wide_result[:, HL : 2 * HL]
        own[2 * p] = a[128:256]
        own[2 * p + 1] = b[128:256]
        both = pair(a[0:128], b[0:128])
        for q in range(CHUNKS):
            sib_out[q, p] = both[q * GROUPS : (q + 1) * GROUPS]

    def send_pre(p):
        for q in range(CHUNKS):
            from_sib[q, p] = copies.one(sib_out.at[q, p], sib_in.at[q, p], sibling)

    def sum_start(q, parts, far, near):
        if q == 0:
            return copies.start([(parts.at[other], far.at[k], x_peers[k]) for k, other in enumerate(xs)], far)
        return copies.one(parts.at[:, 1 - z_lo], near, twin)

    def sum_middle(q, parts, far, near, out, mine, ours, arrival):
        copies.arrive(arrival)
        if q == 0:
            total = ours
            for k in range(3):
                total = total + far[k].astype(F32)
            mine[...] = jnp.where(z_lo == 0, total[0], total[1])
            out[0] = jnp.where(z_lo == 0, total[1], total[0]).astype(BF16)
            return copies.one(out.at[0], near.at[0], twin)
        out[...] = (parts[:, z_lo].astype(F32) + near[...].astype(F32)).astype(BF16)
        group = copies.start(
            [(out.at[other], far.at[k, 0], x_peers[k]) for k, other in enumerate(xs)], far.at[:, 0]
        )
        mine[...] = ours + near[x].astype(F32)
        return group

    def sum_end(q, far, near, mine, arrival):
        copies.arrive(arrival)
        total = mine[...]
        if q == 0:
            return total + near[0].astype(F32)
        for k in range(3):
            total = total + far[k, 0].astype(F32)
        return total

    place = 2 * x + z_lo

    def gather(blocks, steps):
        block = blocks.at[place]
        return copies.start([(block, block, chip_peers[k]) for k in steps], blocks.at[pl.ds(0, len(steps))])

    feature_factor = float(D) ** -0.5
    hidden_factor = float(H) ** -0.5
    factor = float(TOKENS) ** -0.5

    def start_first(q, p):
        copies.arrive(from_sib[q, p])
        a = own[2 * p, q * 64 : (q + 1) * 64].reshape(GROUPS, ROWS, HL)
        b = own[2 * p + 1, q * 64 : (q + 1) * 64].reshape(GROUPS, ROWS, HL)
        both = (jnp.concatenate([a, b], axis=1) + sib_in[q, p].astype(F32)).astype(BF16)
        stage[q, p] = both.reshape(4, 2, 16, HL)
        return sum_start(q, stage.at[q, p], far4.at[q, p], near4.at[q, p])

    def middle_first(q, p, arrivals):
        count = 2 if q == 0 else 1
        group = x * 2 if q == 0 else x * 2 + z_lo
        rows = pl.ds(pl.multiple_of(q * 64 + group * ROWS, ROWS), count * ROWS)
        kept = [own[2 * p + n, rows, :].reshape(count, ROWS, HL) for n in range(2)]
        ours = jnp.concatenate(kept, axis=1) + sib_in[q, p, pl.ds(group, count)].astype(F32)
        if q == 1:
            ours = ours[0]
        return sum_middle(
            q, stage.at[q, p], far4.at[q, p], near4.at[q, p], sum4.at[q, p], mine4.at[q, p], ours, arrivals
        )

    multipliers = []

    def activate(q, arrivals):
        totals = [
            sum_end(q, far4.at[q, p], near4.at[q, p], mine4.at[q, p], arrivals[p]) for p in range(2)
        ]
        gate_tan, up_tan, gate_pre, up_pre = [total[n : n + ROWS] for total in totals for n in (0, ROWS)]
        gate_tan = feature_factor * gate_tan
        up_tan = feature_factor * up_tan
        logistic = jax.nn.sigmoid(gate_pre)
        act = gate_pre * logistic
        slope = logistic * (1.0 + gate_pre * (1.0 - logistic))
        bend = logistic * (1.0 - logistic) * (2.0 + gate_pre * (1.0 - 2.0 * logistic))
        lean = slope * gate_tan
        x_ref[core, q, place] = jnp.concatenate([act * up_pre, lean * up_pre + act * up_tan], axis=0).astype(BF16)
        group = gather(x_ref.at[core, q], range(len(chips)))
        mult[core, q, place] = jnp.concatenate(
            [up_pre * slope, act, up_tan * slope + up_pre * bend * gate_tan, lean], axis=0
        ).astype(BF16)
        block = mult.at[core, q, place]
        multipliers.append(copies.one(block, block, twin))
        return group

    waiting = list(range(CHUNKS))

    def background(count):
        for q in waiting[:count]:
            copies.arrive(multipliers[q])
            block = mult.at[core, q, pl.ds(2 * x, 2)]
            multipliers[q] = copies.start([(block, block, peer) for peer in x_peers], mult.at[core, q, pl.ds(0, 6)])
        del waiting[:count]

    def share_multipliers(q):
        copies.arrive(multipliers[q])
        return copies.one(mult.at[core, q], mult.at[core, q], sibling)

    def output(q, arrival):
        copies.arrive(arrival)
        hidden = x_ref[core, q].reshape(GROUPS * 16, HL)
        result = dot(hidden, wide[...])
        for f in range(2):
            straight = result[:, f * DL : (f + 1) * DL].reshape(GROUPS, 2, ROWS, DL)
            probed = result[:, (f + 2) * DL : (f + 3) * DL].reshape(GROUPS, 2, ROWS, DL)
            outs[q, f] = jnp.concatenate(
                [straight[:, 0], hidden_factor * probed[:, 0] + straight[:, 1]], axis=1
            ).astype(BF16).reshape(2, 4, 16, DL)
        group = copies.start(
            [(outs.at[q, lax.rem(other, 2), lax.div(other, 2)], outs_in.at[q, k], y_peers[k]) for k, other in enumerate(ys)],
            outs_in.at[q],
        )
        return group, copies.one(x_ref.at[core, q], x_ref.at[core, q], sibling)

    half, high = lax.rem(y, 2), lax.div(y, 2)

    def middle(q, arrival):
        copies.arrive(arrival)
        total = outs[q, half, high].astype(F32)
        for k in range(3):
            total += outs_in[q, k].astype(F32)
        mids[q] = total.astype(BF16)
        return copies.start(
            [(mids.at[q, other], mids_in.at[q, k], z_peers[k]) for k, other in enumerate(zs)], mids_in.at[q]
        )

    def cotangent(q, arrival):
        copies.arrive(arrival)
        total = mids[q, z_hi].astype(F32)
        for k in range(3):
            total += mids_in[q, k].astype(F32)
        row = pl.multiple_of(q * 64 + high * 32 + lax.div(z_hi, 2) * 16, 16)
        own_tokens = tok[pl.ds(pl.multiple_of(core * 128 + row, 16), 16), :].astype(F32)
        sib_tokens = tok_sib[pl.ds(row, 16), :].astype(F32)
        chosen = jnp.where(half == 0, own_tokens, sib_tokens)
        chosen = jnp.where(lax.rem(z_hi, 2) == 0, chosen[0:8], chosen[8:16])
        back[q, half, high, z_hi] = jnp.concatenate(
            [factor * (chosen + total[0:8]), factor * total[8:16]], axis=0
        ).astype(BF16)
        block = back.at[q, half, high, z_hi]
        return copies.start([(block, block, peer) for peer in z_peers], back.at[q, half, high, pl.ds(0, 3)])

    def spread(q, arrival):
        copies.arrive(arrival)
        block = back.at[q, half, high]
        return copies.start([(block, block, peer) for peer in y_peers], outs_in.at[q])

    def backward(q, arrival):
        copies.arrive(arrival)
        signals = jnp.concatenate([back[q, f].reshape(GROUPS * 16, DL) for f in range(2)], axis=1)
        straight = dot_last(signals, wide[:, 0 : 2 * DL]).reshape(GROUPS, 2, ROWS, HL)
        probed = dot_last(signals, wide[:, 2 * DL : 4 * DL]).reshape(GROUPS, 2, ROWS, HL)
        both = jnp.concatenate([straight[:, 0], straight[:, 1] + hidden_factor * probed[:, 0]], axis=1)
        hid[q] = both.astype(BF16)
        group = copies.start(
            [(hid.at[q, other], hid_in.at[q, k], chip_peers[k]) for k, other in enumerate(places)], hid_in.at[q]
        )
        shared = copies.one(back.at[q, 1], y_ref.at[core, q], sibling)
        y_ref[core, q] = back[q, 0]
        return group, shared

    parts = (range(0, 4), range(4, 7))

    def pass_on(q, origins):
        blocks = [hids.at[core, q, n] for n in origins]
        return copies.start([(block, block, sibling) for block in blocks], hids.at[core, q, pl.ds(0, len(blocks))])

    def gradients(q, arrival):
        copies.arrive(arrival)
        total = hid[q, place].astype(F32)
        for k in range(len(chips)):
            total += hid_in[q, k].astype(F32)
        hids[core, q, place] = total.astype(BF16)
        return [gather(hids.at[core, q], steps) for steps in parts]

    def combine(side, q, n):
        signals = hids[side, q, n].astype(F32)
        signal, signal_tan = signals[0:8], signals[8:16]
        factors = mult[side, q, n].astype(F32)
        first, second, third, fourth = [factors[m * ROWS : (m + 1) * ROWS] for m in range(4)]
        g_ref[side, q, n] = jnp.concatenate(
            [
                signal * first,
                signal * second,
                signal_tan * first + signal * third,
                signal_tan * second + signal * fourth,
            ],
            axis=0,
        ).astype(BF16)

    def down_products():
        hidden = x_ref[...].reshape(512, HL)
        signals = y_ref[...].astype(F32).reshape(32, 2, ROWS, DL)
        straight = jnp.concatenate([signals[:, 0], jnp.zeros_like(signals[:, 0])], axis=1)
        swapped = jnp.concatenate([signals[:, 1], signals[:, 0]], axis=1)
        dg_ref[...] = dot_rows(hidden, straight.astype(BF16).reshape(512, DL))
        dh_ref[...] = dot_rows(hidden, swapped.astype(BF16).reshape(512, DL))

    def prefetch():
        loads[7].wait()
        loads[8].wait()
        scaled(dw, ds, wide.at[:, pl.ds(0, DL)], HL, DL)
        loads[9].wait()
        theirs = tok.at[pl.ds(pl.multiple_of((1 - core) * 128, 128), 128)]
        return [
            copies.one(wide.at[:, pl.ds(0, DL)], wide.at[:, pl.ds(DL, DL)], sibling),
            copies.one(wide.at[:, pl.ds(2 * DL, DL)], wide.at[:, pl.ds(3 * DL, DL)], sibling),
            copies.one(theirs, tok_sib, sibling),
        ]

    loads[1].wait()
    loads[2].wait()
    pre(0)
    pl.semaphore_wait(barrier, len(partners))
    send_pre(0)
    loads[3].wait()
    loads[4].wait()
    scaled(gw, gs, gw, DL, HL)
    early = [start_first(q, 0) for q in range(CHUNKS)]
    loads[5].wait()
    loads[6].wait()
    scaled(uw, us, uw, DL, HL)
    pre(1)
    send_pre(1)
    shared = []
    prefetched = []

    def first_steps(q):
        groups = early[q], start_first(q, 1)
        if q == 0:
            prefetched.extend(prefetch())
        return groups

    def second_steps(q, arrivals):
        return [middle_first(q, p, arrivals[p]) for p in range(2)]

    def do_output(q, arrivals):
        if q == 0:
            copies.arrive(*prefetched)
        entries, kept = output(q, arrivals)
        shared.append(kept)
        if q == 1:
            background(BACKGROUND[0])
            turned[...] = tok[...].astype(F32).T.astype(BF16)
        return entries

    def do_middle(q, arrivals):
        entries = middle(q, arrivals)
        if q == 1:
            background(BACKGROUND[1])
        return entries

    def do_cotangent(q, arrivals):
        entries = cotangent(q, arrivals)
        if q == 1:
            background(BACKGROUND[2])
        return entries

    def do_backward(q, arrivals):
        entries, kept = backward(q, arrivals)
        shared.append(kept)
        if q == 1:
            shared.extend(share_multipliers(n) for n in range(CHUNKS))
        return entries

    steps = [first_steps, second_steps, activate, do_output, do_middle, do_cotangent, spread, do_backward, gradients]
    flying = [steps[0](q) for q in range(CHUNKS)]
    for step in steps[1:]:
        flying = [step(q, flying[q]) for q in range(CHUNKS)]

    copies.arrive(*shared)
    for q in range(CHUNKS):
        combine(core, q, place)
    down_products()
    copies.sent()
    passed = []
    for q in range(CHUNKS):
        for near in (1, 0):
            origins = [places_from[k] for k in parts[near]]
            copies.arrive(flying[q][near])
            passed.append((q, origins + [place] * near, pass_on(q, origins + [place] * near)))
            for n in origins:
                combine(core, q, n)
    for q, origins, group in passed:
        copies.arrive(group)
        for n in origins:
            combine(1 - core, q, n)
    copies.sent()
    assert len(copies.groups) == GROUPS_SENT


def exchange(*operands):
    vmem = pl.BlockSpec(memory_space=pltpu.VMEM)
    hbm = pl.BlockSpec(memory_space=pltpu.HBM)
    return pl.pallas_call(
        exchange_kernel,
        out_shape=(
            pltpu.VMEM((2, CHUNKS, GROUPS, 32, HL), BF16),
            pltpu.VMEM((HL, DL), F32),
            pltpu.VMEM((HL, DL), F32),
            pltpu.VMEM((DL, 256), BF16),
        ),
        in_specs=[hbm] * 10,
        out_specs=(vmem, vmem, vmem, vmem),
        scratch_shapes=[
            pltpu.VMEM((256, DL), BF16),
            pltpu.VMEM((128, DL), BF16),
            pltpu.VMEM((256, DL), BF16),
            pltpu.VMEM((2, DL, 2 * HL), BF16),
            pltpu.VMEM((HL, DL), BF16),
            pltpu.VMEM((HL, 4 * DL), BF16),
            pltpu.VMEM((DL,), F32),
            pltpu.VMEM((DL,), F32),
            pltpu.VMEM((HL,), F32),
            pltpu.VMEM((CHUNKS, 2, GROUPS, 16, HL), BF16),
            pltpu.VMEM((CHUNKS, 2, GROUPS, 16, HL), BF16),
            pltpu.VMEM((4, 128, HL), F32),
            pltpu.VMEM((CHUNKS, 2, 4, 2, 16, HL), BF16),
            pltpu.VMEM((CHUNKS, 2, 3, 2, 16, HL), BF16),
            pltpu.VMEM((CHUNKS, 2, 4, 16, HL), BF16),
            pltpu.VMEM((CHUNKS, 2, 4, 16, HL), BF16),
            pltpu.VMEM((CHUNKS, 2, 16, HL), F32),
            pltpu.VMEM((2, CHUNKS, GROUPS, 16, HL), BF16),
            pltpu.VMEM((2, CHUNKS, 2, 4, 16, DL), BF16),
            pltpu.VMEM((2, CHUNKS, GROUPS, 16, HL), BF16),
            pltpu.VMEM((2, CHUNKS, GROUPS, 32, HL), BF16),
            pltpu.VMEM((CHUNKS, 2, 2, 4, 16, DL), BF16),
            pltpu.VMEM((CHUNKS, 3, 4, 16, DL), BF16),
            pltpu.VMEM((CHUNKS, 4, 16, DL), BF16),
            pltpu.VMEM((CHUNKS, 3, 16, DL), BF16),
            pltpu.VMEM((CHUNKS, 2, 2, 4, 16, DL), BF16),
            pltpu.VMEM((CHUNKS, GROUPS, 16, HL), BF16),
            pltpu.VMEM((CHUNKS, len(ZERO_STEPS), 16, HL), BF16),
            pltpu.SemaphoreType.DMA((10,)),
            pltpu.SemaphoreType.DMA((SENDS,)),
            pltpu.SemaphoreType.DMA((GROUPS_SENT,)),
        ],
        compiler_params=pltpu.CompilerParams(
            collective_id=0, has_side_effects=True, vmem_limit_bytes=44 * 2**20
        ),
        name="exchange",
    )(*[pltpu.with_memory_space_constraint(operand, pltpu.HBM) for operand in operands])


def products_kernel(turned, g, down, down_tan, gg, ug, dg, gh, uh, dh, square, sems):
    copies = []

    def put(src, out, first, count):
        rows = pl.ds(first, count)
        copy = pltpu.make_async_copy(src.at[rows], out.at[rows], sems.at[len(copies)])
        copy.start()
        copies.append(copy)

    for src, out in ((down, dg), (down_tan, dh)):
        for half in range(2):
            put(src, out, half * (HL // 2), HL // 2)
    for n, out in enumerate((gg, ug, gh, uh)):
        part = g[:, :, :, (n // 2) * 16 : (n // 2) * 16 + 16, :].astype(F32).reshape(32, 2, ROWS, HL)
        rows = part[:, n % 2].reshape(256, HL).astype(BF16)
        for half in range(2):
            first = half * (DL // 2)
            square[n, first : first + DL // 2] = dot(turned[first : first + DL // 2], rows)
            put(square.at[n], out, first, DL // 2)
    for copy in copies:
        copy.wait()


def products(turned, g, down, down_tan):
    vmem = pl.BlockSpec(memory_space=pltpu.VMEM)
    hbm = pl.BlockSpec(memory_space=pl.ANY)
    tall = jax.ShapeDtypeStruct((DL, HL), F32)
    flat = jax.ShapeDtypeStruct((HL, DL), F32)
    return pl.pallas_call(
        products_kernel,
        out_shape=(tall, tall, flat, tall, tall, flat),
        in_specs=[vmem] * 4,
        out_specs=[hbm] * 6,
        scratch_shapes=[pltpu.VMEM((4, DL, HL), F32), pltpu.SemaphoreType.DMA((12,))],
        compiler_params=pltpu.CompilerParams(vmem_limit_bytes=40 * 2**20),
        name="products",
    )(turned, g, down, down_tan)


def local(
    tokens, gate_weight, up_weight, down_weight, gate_scale, up_scale, down_scale, gate_probe, up_probe, down_probe
):
    g, down, down_tan, turned = exchange(
        tokens, gate_weight, up_weight, down_weight, gate_probe, up_probe, down_probe,
        gate_scale, up_scale, down_scale,
    )
    return products(turned, g, down, down_tan)


def solution(mesh):
    in_specs = (
        P(None, "zero"),
        P("zero", "rep"),
        P("zero", "rep"),
        P("rep", "zero"),
        P("zero"),
        P("zero"),
        P("rep"),
        P("zero", "rep"),
        P("zero", "rep"),
        P("rep", "zero"),
    )
    out_specs = (
        P("zero", "rep"),
        P("zero", "rep"),
        P("rep", "zero"),
        P("zero", "rep"),
        P("zero", "rep"),
        P("rep", "zero"),
    )
    return jax.shard_map(local, mesh=mesh, in_specs=in_specs, out_specs=out_specs, check_vma=False)
```

time: 68.1 us -> 64.1 us (0.941)
  Pallas kernels: 67.4 us -> 63.4 us
    pallas_call x1, Pallas kernels: 64 us -> 60 us  [exchange(): pl.pallas_call(exchange_kernel, out_shape=(pltpu.VMEM((2, CHUNKS, GROUPS,...]
where the time goes in v3:
time: 64.1 us; the launch traced here: 64 us
  Pallas kernels  63.4 us (99%)
    pallas_call x1, Pallas kernels, exchange(): pl.pallas_call(exchange_kernel, out_shape=(pltpu.VMEM((2, CHUNKS, GROUPS,...  60 us
    pallas_call x1, Pallas kernels, products(): pl.pallas_call(products_kernel, out_shape=(tall, tall, flat, tall, tall,...  3.38 us

profile of v3, /device:TPU:1, one launch (start us, length us, event | category | flops | bytes accessed | tf_op | source)
XLA Modules:
  0.0 64.0 jit_solution(507094518722554713)
XLA Ops:
  0.6 60.0 %exchange.1 = (bf16[2,2,8,32,896]{4,3,2,1,0:T(8,128)(2,1)S(1)}, f32[896,384]{1,0:T(8,128)S(1)}, f32[896,384]{1,0:T(8,128)S(1)}, bf16[384,256]{1,0:T(8,128)(2,1)S(1)}) custom-call(bf16[256,384]{1,0:T(8,128)(2,1)} %tok_hbm.1, bf16[384,896]{1,0:T(8,128)(2,1)} %gw_hbm.1, bf16[384,896]{1,0:T(8,128)(2,1)} %uw_hbm.1, bf16[896,384]{1,0:T(8,128)(2,1)} %dw_hbm.1, ...), custom_call_target="tpu_custom_call" | custom-call | tf_op jit(solution)/shard_map/exchange/pallas_call | solution.py:448
  60.6 3.4 %products.1 = (f32[384,896]{1,0:T(8,128)}, f32[384,896]{1,0:T(8,128)}, f32[896,384]{1,0:T(8,128)}, f32[384,896]{1,0:T(8,128)}, f32[384,896]{1,0:T(8,128)}, /*index=5*/f32[896,384]{1,0:T(8,128)}) custom-call(bf16[384,256]{1,0:T(8,128)(2,1)S(1)} %get-tuple-element.10.turned, bf16[2,2,8,32,896]{4,3,2,1,0:T(8,128)(2,1)S(1)} %get-tuple-element.11.g, ...), custom_call_target="tpu_custom_call" | custom-call | tf_op jit(solution)/shard_map/products/pallas_call | solution.py:526

commit v4 on v3

--- a/solution.py
+++ b/solution.py
@@ -16,7 +16,7 @@
 CHUNKS = 2
 GROUPS = 8
 ROWS = 8
-BACKGROUND = (1, 1, 0)
+BACKGROUND = (1, 1)
 GROUPS_SENT = 45
 SENDS = 12
 
@@ -88,7 +88,7 @@
     sib_out, sib_in, own, stage, far4, near4, sum4, mine4,
     x_ref, y_ref, hids, mult, outs, outs_in, mids, mids_in, back,
     hid, hid_in,
-    load_sem, send_sem, recv_sem,
+    load_sem, send_sem, recv_sem, ready,
 ):
     rep = lax.axis_index("rep")
     zero = lax.axis_index("zero")
@@ -110,7 +110,7 @@
     places = [2 * other_x + other_z for other_x, other_z in chips]
     places_from = [2 * other_x + other_z for other_x, other_z in chips_from]
     chip_peers = [(rep, other_z * 8 + other_x * 2 + core) for other_x, other_z in chips]
-    partners = [sibling] + chip_peers + y_peers + z_peers
+    partners = [sibling, twin] + x_peers + y_peers + z_peers[1:]
     copies = Copies(send_sem, recv_sem, sibling)
 
     barrier = pltpu.get_barrier_semaphore()
@@ -232,9 +232,11 @@
         mult[core, q, place] = jnp.concatenate(
             [up_pre * slope, act, up_tan * slope + up_pre * bend * gate_tan, lean], axis=0
         ).astype(BF16)
+        return group
+
+    def start_multipliers(q):
         block = mult.at[core, q, place]
         multipliers.append(copies.one(block, block, twin))
-        return group
 
     waiting = list(range(CHUNKS))
 
@@ -263,7 +265,7 @@
             [(outs.at[q, lax.rem(other, 2), lax.div(other, 2)], outs_in.at[q, k], y_peers[k]) for k, other in enumerate(ys)],
             outs_in.at[q],
         )
-        return group, copies.one(x_ref.at[core, q], x_ref.at[core, q], sibling)
+        return group
 
     half, high = lax.rem(y, 2), lax.div(y, 2)
 
@@ -308,9 +310,11 @@
         group = copies.start(
             [(hid.at[q, other], hid_in.at[q, k], chip_peers[k]) for k, other in enumerate(places)], hid_in.at[q]
         )
-        shared = copies.one(back.at[q, 1], y_ref.at[core, q], sibling)
+        return group
+
+    def share_signals(q):
         y_ref[core, q] = back[q, 0]
-        return group, shared
+        return copies.one(back.at[q, 1], y_ref.at[core, q], sibling)
 
     parts = (range(0, 4), range(4, 7))
 
@@ -365,6 +369,8 @@
     loads[2].wait()
     pre(0)
     pl.semaphore_wait(barrier, len(partners))
+    for other in z_peers[1:]:
+        pl.semaphore_signal(ready, inc=1, device_id=other, device_id_type=MESH)
     send_pre(0)
     loads[3].wait()
     loads[4].wait()
@@ -380,7 +386,7 @@
 
     def first_steps(q):
         groups = early[q], start_first(q, 1)
-        if q == 0:
+        if q == 1:
             prefetched.extend(prefetch())
         return groups
 
@@ -390,33 +396,42 @@
     def do_output(q, arrivals):
         if q == 0:
             copies.arrive(*prefetched)
-        entries, kept = output(q, arrivals)
-        shared.append(kept)
-        if q == 1:
-            background(BACKGROUND[0])
+        entries = output(q, arrivals)
+        if q == 1:
+            for n in range(CHUNKS):
+                start_multipliers(n)
+            shared.extend(copies.one(x_ref.at[core, n], x_ref.at[core, n], sibling) for n in range(CHUNKS))
             turned[...] = tok[...].astype(F32).T.astype(BF16)
         return entries
 
     def do_middle(q, arrivals):
+        if q == 0:
+            pl.semaphore_wait(ready, 2)
         entries = middle(q, arrivals)
+        if q == 1:
+            background(BACKGROUND[0])
+        return entries
+
+    def do_cotangent(q, arrivals):
+        entries = cotangent(q, arrivals)
         if q == 1:
             background(BACKGROUND[1])
         return entries
 
-    def do_cotangent(q, arrivals):
-        entries = cotangent(q, arrivals)
-        if q == 1:
-            background(BACKGROUND[2])
+    def do_spread(q, arrivals):
+        group = spread(q, arrivals)
+        if q == 1:
+            shared.append(share_multipliers(0))
+        return group
+
+    def do_backward(q, arrivals):
+        entries = backward(q, arrivals)
+        if q == 1:
+            shared.extend(share_signals(n) for n in range(CHUNKS))
+            shared.append(share_multipliers(1))
         return entries
 
-    def do_backward(q, arrivals):
-        entries, kept = backward(q, arrivals)
-        shared.append(kept)
-        if q == 1:
-            shared.extend(share_multipliers(n) for n in range(CHUNKS))
-        return entries
-
-    steps = [first_steps, second_steps, activate, do_output, do_middle, do_cotangent, spread, do_backward, gradients]
+    steps = [first_steps, second_steps, activate, do_output, do_middle, do_cotangent, do_spread, do_backward, gradients]
     flying = [steps[0](q) for q in range(CHUNKS)]
     for step in steps[1:]:
         flying = [step(q, flying[q]) for q in range(CHUNKS)]
@@ -487,6 +502,7 @@
             pltpu.SemaphoreType.DMA((10,)),
             pltpu.SemaphoreType.DMA((SENDS,)),
             pltpu.SemaphoreType.DMA((GROUPS_SENT,)),
+            pltpu.SemaphoreType.REGULAR,
         ],
         compiler_params=pltpu.CompilerParams(
             collective_id=0, has_side_effects=True, vmem_limit_bytes=44 * 2**20

time: 64.1 us -> 63.3 us (0.988)
  Pallas kernels: 63.4 us -> 62.6 us
    pallas_call x1, Pallas kernels: 60 us -> 59.2 us  [exchange(): pl.pallas_call(exchange_kernel, out_shape=(pltpu.VMEM((2, CHUNKS, GROUPS,...]
where the time goes in v4:
time: 63.3 us; the launch traced here: 63.2 us
  Pallas kernels  62.6 us (99%)
  between operations  0.64 us (1%)
    pallas_call x1, Pallas kernels, exchange(): pl.pallas_call(exchange_kernel, out_shape=(pltpu.VMEM((2, CHUNKS, GROUPS,...  59.2 us
    pallas_call x1, Pallas kernels, products(): pl.pallas_call(products_kernel, out_shape=(tall, tall, flat, tall, tall,...  3.38 us

profile of v4, /device:TPU:1, one launch (start us, length us, event | category | flops | bytes accessed | tf_op | source)
XLA Modules:
  0.0 63.2 jit_solution(12594554026042622204)
XLA Ops:
  0.6 59.2 %exchange.1 = (bf16[2,2,8,32,896]{4,3,2,1,0:T(8,128)(2,1)S(1)}, f32[896,384]{1,0:T(8,128)S(1)}, f32[896,384]{1,0:T(8,128)S(1)}, bf16[384,256]{1,0:T(8,128)(2,1)S(1)}) custom-call(bf16[256,384]{1,0:T(8,128)(2,1)} %tok_hbm.1, bf16[384,896]{1,0:T(8,128)(2,1)} %gw_hbm.1, bf16[384,896]{1,0:T(8,128)(2,1)} %uw_hbm.1, bf16[896,384]{1,0:T(8,128)(2,1)} %dw_hbm.1, ...), custom_call_target="tpu_custom_call" | custom-call | tf_op jit(solution)/shard_map/exchange/pallas_call | solution.py:463
  59.8 3.4 %products.1 = (f32[384,896]{1,0:T(8,128)}, f32[384,896]{1,0:T(8,128)}, f32[896,384]{1,0:T(8,128)}, f32[384,896]{1,0:T(8,128)}, f32[384,896]{1,0:T(8,128)}, /*index=5*/f32[896,384]{1,0:T(8,128)}) custom-call(bf16[384,256]{1,0:T(8,128)(2,1)S(1)} %get-tuple-element.10.turned, bf16[2,2,8,32,896]{4,3,2,1,0:T(8,128)(2,1)S(1)} %get-tuple-element.11.g, ...), custom_call_target="tpu_custom_call" | custom-call | tf_op jit(solution)/shard_map/products/pallas_call | solution.py:542

commit v5 on v4

--- a/solution.py
+++ b/solution.py
@@ -390,9 +390,6 @@
             prefetched.extend(prefetch())
         return groups
 
-    def second_steps(q, arrivals):
-        return [middle_first(q, p, arrivals[p]) for p in range(2)]
-
     def do_output(q, arrivals):
         if q == 0:
             copies.arrive(*prefetched)
@@ -431,9 +428,13 @@
             shared.append(share_multipliers(1))
         return entries
 
-    steps = [first_steps, second_steps, activate, do_output, do_middle, do_cotangent, do_spread, do_backward, gradients]
-    flying = [steps[0](q) for q in range(CHUNKS)]
-    for step in steps[1:]:
+    steps = [activate, do_output, do_middle, do_cotangent, do_spread, do_backward, gradients]
+    begun = [first_steps(q) for q in range(CHUNKS)]
+    flying = [[], []]
+    for p in range(2):
+        for q in range(CHUNKS):
+            flying[q].append(middle_first(q, p, begun[q][p]))
+    for step in steps:
         flying = [step(q, flying[q]) for q in range(CHUNKS)]
 
     copies.arrive(*shared)
@@ -442,8 +443,8 @@
     down_products()
     copies.sent()
     passed = []
-    for q in range(CHUNKS):
-        for near in (1, 0):
+    for near in (1, 0):
+        for q in range(CHUNKS):
             origins = [places_from[k] for k in parts[near]]
             copies.arrive(flying[q][near])
             passed.append((q, origins + [place] * near, pass_on(q, origins + [place] * near)))

time: 63.3 us -> 62.4 us (0.986)
  Pallas kernels: 62.6 us -> 61.7 us
    pallas_call x1, Pallas kernels: 59.2 us -> 58.3 us  [exchange(): pl.pallas_call(exchange_kernel, out_shape=(pltpu.VMEM((2, CHUNKS, GROUPS,...]
where the time goes in v5:
time: 62.4 us; the launch traced here: 62.3 us
  Pallas kernels  61.7 us (99%)
  between operations  0.64 us (1%)
    pallas_call x1, Pallas kernels, exchange(): pl.pallas_call(exchange_kernel, out_shape=(pltpu.VMEM((2, CHUNKS, GROUPS,...  58.3 us
    pallas_call x1, Pallas kernels, products(): pl.pallas_call(products_kernel, out_shape=(tall, tall, flat, tall, tall,...  3.38 us

profile of v5, /device:TPU:1, one launch (start us, length us, event | category | flops | bytes accessed | tf_op | source)
XLA Modules:
  0.0 62.3 jit_solution(7810776900080652099)
XLA Ops:
  0.6 58.3 %exchange.1 = (bf16[2,2,8,32,896]{4,3,2,1,0:T(8,128)(2,1)S(1)}, f32[896,384]{1,0:T(8,128)S(1)}, f32[896,384]{1,0:T(8,128)S(1)}, bf16[384,256]{1,0:T(8,128)(2,1)S(1)}) custom-call(bf16[256,384]{1,0:T(8,128)(2,1)} %tok_hbm.1, bf16[384,896]{1,0:T(8,128)(2,1)} %gw_hbm.1, bf16[384,896]{1,0:T(8,128)(2,1)} %uw_hbm.1, bf16[896,384]{1,0:T(8,128)(2,1)} %dw_hbm.1, ...), custom_call_target="tpu_custom_call" | custom-call | tf_op jit(solution)/shard_map/exchange/pallas_call | solution.py:464
  59.0 3.4 %products.1 = (f32[384,896]{1,0:T(8,128)}, f32[384,896]{1,0:T(8,128)}, f32[896,384]{1,0:T(8,128)}, f32[384,896]{1,0:T(8,128)}, f32[384,896]{1,0:T(8,128)}, /*index=5*/f32[896,384]{1,0:T(8,128)}) custom-call(bf16[384,256]{1,0:T(8,128)(2,1)S(1)} %get-tuple-element.10.turned, bf16[2,2,8,32,896]{4,3,2,1,0:T(8,128)(2,1)S(1)} %get-tuple-element.11.g, ...), custom_call_target="tpu_custom_call" | custom-call | tf_op jit(solution)/shard_map/products/pallas_call | solution.py:543

commit v6 on v5

--- a/solution.py
+++ b/solution.py
@@ -17,7 +17,7 @@
 GROUPS = 8
 ROWS = 8
 BACKGROUND = (1, 1)
-GROUPS_SENT = 45
+GROUPS_SENT = 49
 SENDS = 12
 
 BF16 = jnp.bfloat16
@@ -316,7 +316,7 @@
         y_ref[core, q] = back[q, 0]
         return copies.one(back.at[q, 1], y_ref.at[core, q], sibling)
 
-    parts = (range(0, 4), range(4, 7))
+    parts = (range(0, 2), range(2, 4), range(4, 7))
 
     def pass_on(q, origins):
         blocks = [hids.at[core, q, n] for n in origins]
@@ -443,11 +443,11 @@
     down_products()
     copies.sent()
     passed = []
-    for near in (1, 0):
+    for near in (2, 1, 0):
         for q in range(CHUNKS):
             origins = [places_from[k] for k in parts[near]]
             copies.arrive(flying[q][near])
-            passed.append((q, origins + [place] * near, pass_on(q, origins + [place] * near)))
+            passed.append((q, origins + [place] * (near == 2), pass_on(q, origins + [place] * (near == 2))))
             for n in origins:
                 combine(core, q, n)
     for q, origins, group in passed:

time: 62.4 us -> 62.4 us (level)
  no operation moved by 1% of the time
where the time goes in v6:
time: 62.4 us; the launch traced here: 62.3 us
  Pallas kernels  61.6 us (99%)
  between operations  0.64 us (1%)
    pallas_call x1, Pallas kernels, exchange(): pl.pallas_call(exchange_kernel, out_shape=(pltpu.VMEM((2, CHUNKS, GROUPS,...  58.2 us
    pallas_call x1, Pallas kernels, products(): pl.pallas_call(products_kernel, out_shape=(tall, tall, flat, tall, tall,...  3.38 us

profile of v6, /device:TPU:1, one launch (start us, length us, event | category | flops | bytes accessed | tf_op | source)
XLA Modules:
  0.0 62.3 jit_solution(15391694964826685868)
XLA Ops:
  0.6 58.2 %exchange.1 = (bf16[2,2,8,32,896]{4,3,2,1,0:T(8,128)(2,1)S(1)}, f32[896,384]{1,0:T(8,128)S(1)}, f32[896,384]{1,0:T(8,128)S(1)}, bf16[384,256]{1,0:T(8,128)(2,1)S(1)}) custom-call(bf16[256,384]{1,0:T(8,128)(2,1)} %tok_hbm.1, bf16[384,896]{1,0:T(8,128)(2,1)} %gw_hbm.1, bf16[384,896]{1,0:T(8,128)(2,1)} %uw_hbm.1, bf16[896,384]{1,0:T(8,128)(2,1)} %dw_hbm.1, ...), custom_call_target="tpu_custom_call" | custom-call | tf_op jit(solution)/shard_map/exchange/pallas_call | solution.py:464
  58.9 3.4 %products.1 = (f32[384,896]{1,0:T(8,128)}, f32[384,896]{1,0:T(8,128)}, f32[896,384]{1,0:T(8,128)}, f32[384,896]{1,0:T(8,128)}, f32[384,896]{1,0:T(8,128)}, /*index=5*/f32[896,384]{1,0:T(8,128)}) custom-call(bf16[384,256]{1,0:T(8,128)(2,1)S(1)} %get-tuple-element.10.turned, bf16[2,2,8,32,896]{4,3,2,1,0:T(8,128)(2,1)S(1)} %get-tuple-element.11.g, ...), custom_call_target="tpu_custom_call" | custom-call | tf_op jit(solution)/shard_map/products/pallas_call | solution.py:543
